TPU v7x, 128 devices: a whole 4x4x4 slice. The times are simulated.
128 devices in a mesh: dp: 32 (over x, y, z_lo), seq: 4 (over z_hi, core).
Axes of the slice: x: 4, y: 4, z: 4 (z_hi: 2, z_lo: 2; z = z_hi * 2 + z_lo), core: 2. Of those that a mesh axis runs over, the one named last changes fastest.
Arguments:
- block_in: bfloat16 [32, 1024, 768], P('dp', 'seq'), may hold values from -6 to 6
- cotangent: bfloat16 [32, 1024, 768], P('dp', 'seq'), may hold values from -6 to 6
- attn_gain: bfloat16 [768], P('dp'), may hold values from 0.099609375 to 1.8984375
- attn_bias: bfloat16 [768], P('dp'), may hold values from -3 to 3
- mlp_gain: bfloat16 [768], P('dp'), may hold values from 0.099609375 to 1.8984375
- mlp_bias: bfloat16 [768], P('dp'), may hold values from -3 to 3
- qkv_weight: bfloat16 [768, 2304], P('dp'), may hold values from -0.21875 to 0.21875
- qkv_bias: bfloat16 [2304], P('dp'), may hold values from -3 to 3
- proj_weight: bfloat16 [768, 768], P('dp'), may hold values from -2.5 to 2.5
- proj_bias: bfloat16 [768], P('dp'), may hold values from -3 to 3
- up_weight: bfloat16 [768, 3072], P('dp'), may hold values from -0.21875 to 0.21875
- up_bias: bfloat16 [3072], P('dp'), may hold values from -3 to 3
- down_weight: bfloat16 [3072, 768], P('dp'), may hold values from -0.109375 to 0.109375
- down_bias: bfloat16 [768], P('dp'), may hold values from -3 to 3
Outputs:
- block_out: bfloat16 [32, 1024, 768], P('dp', 'seq')
- input_grad: bfloat16 [32, 1024, 768], P('dp', 'seq')
- attn_gain_grad: float32 [768], P('dp')
- attn_bias_grad: float32 [768], P('dp')
- mlp_gain_grad: float32 [768], P('dp')
- mlp_bias_grad: float32 [768], P('dp')
- qkv_weight_grad: float32 [768, 2304], P('dp')
- qkv_bias_grad: float32 [2304], P('dp')
- proj_weight_grad: float32 [768, 768], P('dp')
- proj_bias_grad: float32 [768], P('dp')
- up_weight_grad: float32 [768, 3072], P('dp')
- up_bias_grad: float32 [3072], P('dp')
- down_weight_grad: float32 [3072, 768], P('dp')
- down_bias_grad: float32 [768], P('dp')
All inputs are finite; a program needn't handle non-finite values.
Results may differ from a plain program's by a relative error of at most 0.025.
Values may be sent and summed in bfloat16 or wider, within the bound.
A program may use at most 128 MiB of HBM per device.

v0:
```python
import math

import jax
import jax.numpy as jnp
from jax import lax
from jax.sharding import PartitionSpec as P

HEADS = 12
HEAD_DIM = 64
ROT_DIM = 16


EPSILON = 1e-05
MASKED = -1e30


def as_sent(array):

    def short(part):
        return part.astype(jnp.bfloat16) if part.dtype == jnp.float32 else part

    return jax.tree.map(short, array)


def normalize(values):
    center = values - jnp.mean(values, axis=-1, keepdims=True)
    inv_std = lax.rsqrt(jnp.mean(center * center, axis=-1, keepdims=True) + EPSILON)
    return (center * inv_std, inv_std)


def norm_back(grad_norm, normed, inv_std):
    return inv_std * (
        grad_norm
        - jnp.mean(grad_norm, axis=-1, keepdims=True)
        - normed * jnp.mean(grad_norm * normed, axis=-1, keepdims=True)
    )


def tables(positions, rot_dims):
    half_dims = rot_dims // 2
    freqs = jnp.power(10000.0, -2.0 * jnp.arange(half_dims, dtype=jnp.float32) / rot_dims)
    angles = positions.astype(jnp.float32)[:, None] * freqs[None, :]
    angles = jnp.concatenate([angles, angles], axis=-1)
    return (jnp.cos(angles), jnp.sin(angles))


def turn(part, cosine, sine):
    half_dims = part.shape[-1] // 2
    swapped = jnp.concatenate([-part[..., half_dims:], part[..., :half_dims]], axis=-1)
    return part * cosine + swapped * sine


def turn_back(grad_part, cosine, sine):
    half_dims = grad_part.shape[-1] // 2
    scaled = grad_part * sine
    swapped = jnp.concatenate([scaled[..., half_dims:], -scaled[..., :half_dims]], axis=-1)
    return grad_part * cosine + swapped


def apply_turn(packed, cosine, sine, method, rot_dims):
    paired = packed[..., :2, :]
    turned = jnp.concatenate(
        [method(paired[..., :rot_dims], cosine, sine), paired[..., rot_dims:]], axis=-1
    )
    return jnp.concatenate([turned, packed[..., 2:, :]], axis=-2)


def gelu_slope(values):
    normal_cdf = 0.5 * (1.0 + lax.erf(values * (1.0 / math.sqrt(2.0))))
    density = jnp.exp(-0.5 * values * values) * (1.0 / math.sqrt(2.0 * math.pi))
    return normal_cdf + values * density


def scores_of(query_rows, key_rows, start, scale):
    scores = (
        jnp.einsum("qhd,khd->hqk", query_rows, key_rows, preferred_element_type=jnp.float32) * scale
    )
    row_place = start + jnp.arange(query_rows.shape[0])
    col_place = jnp.arange(key_rows.shape[0])
    allowed = row_place[:, None] >= col_place[None, :]
    return jnp.where(allowed[None, :, :], scores, MASKED)


def attend_one(packed):
    length = packed.shape[0]
    queries = packed[:, :, 0, :]
    key_rows = packed[:, :, 1, :]
    value_rows = packed[:, :, 2, :]
    scale = 1.0 / math.sqrt(packed.shape[-1])
    span = min(512, length)
    outputs = []
    log_sums = []
    for row_block in range(length // span):
        start = row_block * span
        finish = start + span
        scores = scores_of(queries[start:finish], key_rows[:finish], start, scale)
        peak = jnp.max(scores, axis=-1, keepdims=True)
        expo = jnp.exp(scores - peak)
        total = jnp.sum(expo, axis=-1, keepdims=True)
        probs = (expo / total).astype(jnp.bfloat16)
        outputs.append(
            jnp.einsum(
                "hqk,khd->qhd", probs, value_rows[:finish], preferred_element_type=jnp.float32
            )
        )
        log_sums.append((peak + jnp.log(total))[..., 0])
    return (
        jnp.concatenate(outputs, axis=0).astype(jnp.bfloat16),
        jnp.concatenate(log_sums, axis=-1),
    )


def attend_back(operands):
    packed, grad_rows, log_sum = operands
    length = packed.shape[0]
    queries = packed[:, :, 0, :]
    key_rows = packed[:, :, 1, :]
    value_rows = packed[:, :, 2, :]
    scale = 1.0 / math.sqrt(packed.shape[-1])
    span = min(512, length)
    grad_queries = []
    grad_keys = jnp.zeros(queries.shape, jnp.float32)
    grad_values = jnp.zeros(queries.shape, jnp.float32)
    for row_block in range(length // span):
        start = row_block * span
        finish = start + span
        scores = scores_of(queries[start:finish], key_rows[:finish], start, scale)
        probs = jnp.exp(scores - log_sum[:, start:finish, None])
        grad_probs = jnp.einsum(
            "qhd,khd->hqk",
            grad_rows[start:finish],
            value_rows[:finish],
            preferred_element_type=jnp.float32,
        )
        inner = jnp.sum(probs * grad_probs, axis=-1, keepdims=True)
        grad_scores = (probs * (grad_probs - inner)).astype(jnp.bfloat16)
        grad_queries.append(
            jnp.einsum(
                "hqk,khd->qhd", grad_scores, key_rows[:finish], preferred_element_type=jnp.float32
            )
            * scale
        )
        grad_keys = grad_keys.at[:finish].add(
            jnp.einsum(
                "hqk,qhd->khd",
                grad_scores,
                queries[start:finish],
                preferred_element_type=jnp.float32,
            )
            * scale
        )
        grad_values = grad_values.at[:finish].add(
            jnp.einsum(
                "hqk,qhd->khd",
                probs.astype(jnp.bfloat16),
                grad_rows[start:finish],
                preferred_element_type=jnp.float32,
            )
        )
    stacked = jnp.stack([jnp.concatenate(grad_queries, axis=0), grad_keys, grad_values], axis=2)
    return stacked.astype(jnp.bfloat16)


def flat_rows(values):
    return values.reshape(-1, values.shape[-1])


def outer_sum(left, right):
    return jnp.einsum(
        "rd,re->de", flat_rows(left), flat_rows(right), preferred_element_type=jnp.float32
    )


def row_total(values):
    return jnp.sum(flat_rows(values).astype(jnp.float32), axis=0)


def local(
    block_in,
    cotangent,
    attn_gain,
    attn_bias,
    mlp_gain,
    mlp_bias,
    qkv_weight,
    qkv_bias,
    proj_weight,
    proj_bias,
    up_weight,
    up_bias,
    down_weight,
    down_bias,
):
    shards = (
        attn_gain,
        attn_bias,
        mlp_gain,
        mlp_bias,
        qkv_weight,
        qkv_bias,
        proj_weight,
        proj_bias,
        up_weight,
        up_bias,
        down_weight,
        down_bias,
    )
    gathered = (
        lax.all_gather(shards[0], "dp", axis=0, tiled=True),
        lax.all_gather(shards[1], "dp", axis=0, tiled=True),
        lax.all_gather(shards[2], "dp", axis=0, tiled=True),
        lax.all_gather(shards[3], "dp", axis=0, tiled=True),
        lax.all_gather(shards[4], "dp", axis=0, tiled=True),
        lax.all_gather(shards[5], "dp", axis=0, tiled=True),
        lax.all_gather(shards[6], "dp", axis=0, tiled=True),
        lax.all_gather(shards[7], "dp", axis=0, tiled=True),
        lax.all_gather(shards[8], "dp", axis=0, tiled=True),
        lax.all_gather(shards[9], "dp", axis=0, tiled=True),
        lax.all_gather(shards[10], "dp", axis=0, tiled=True),
        lax.all_gather(shards[11], "dp", axis=0, tiled=True),
    )
    (
        gain_attn,
        bias_attn,
        gain_mlp,
        bias_mlp,
        w_qkv,
        b_qkv,
        w_proj,
        b_proj,
        w_up,
        b_up,
        w_down,
        b_down,
    ) = gathered
    seqs_here, local_len, width = block_in.shape
    groups = lax.axis_size("seq")
    heads_local = HEADS // groups
    full_len = local_len * groups
    inputs = block_in.astype(jnp.float32)
    normed, inv_std = normalize(inputs)
    in_attn = (normed * gain_attn + bias_attn).astype(jnp.bfloat16)
    in_mlp = (normed * gain_mlp + bias_mlp).astype(jnp.bfloat16)
    qkv_pre = (jnp.dot(in_attn, w_qkv, preferred_element_type=jnp.float32) + b_qkv).reshape(
        seqs_here, local_len, HEADS, 3, HEAD_DIM
    )
    positions = lax.axis_index("seq") * local_len + jnp.arange(local_len)
    cosine, sine = tables(positions, ROT_DIM)
    cosine = cosine[:, None, None, :]
    sine = sine[:, None, None, :]
    turned = apply_turn(qkv_pre, cosine, sine, turn, ROT_DIM).astype(jnp.bfloat16)
    turned = turned.reshape(seqs_here, local_len, groups, heads_local * 3 * HEAD_DIM)
    head_rows = lax.all_to_all(turned, "seq", split_axis=2, concat_axis=1, tiled=True).reshape(
        seqs_here, full_len, heads_local, 3, HEAD_DIM
    )
    att_heads, log_sums = lax.map(attend_one, head_rows)
    att_tokens = lax.all_to_all(
        as_sent(att_heads.reshape(seqs_here, full_len, 1, heads_local * HEAD_DIM)),
        "seq",
        split_axis=1,
        concat_axis=2,
        tiled=True,
    )
    att_tokens = att_tokens.reshape(seqs_here, local_len, width)
    attn_out = jnp.dot(att_tokens, w_proj, preferred_element_type=jnp.float32) + b_proj
    up_pre = jnp.dot(in_mlp, w_up, preferred_element_type=jnp.float32) + b_up
    activ = jax.nn.gelu(up_pre, approximate=False).astype(jnp.bfloat16)
    mlp_out = jnp.dot(activ, w_down, preferred_element_type=jnp.float32) + b_down
    block_out = (inputs + attn_out + mlp_out).astype(jnp.bfloat16)
    again = (
        lax.all_gather(attn_gain, "dp", axis=0, tiled=True),
        lax.all_gather(mlp_gain, "dp", axis=0, tiled=True),
        lax.all_gather(qkv_weight, "dp", axis=0, tiled=True),
        lax.all_gather(proj_weight, "dp", axis=0, tiled=True),
        lax.all_gather(up_weight, "dp", axis=0, tiled=True),
        lax.all_gather(down_weight, "dp", axis=0, tiled=True),
    )
    (
        gain_attn_b,
        gain_mlp_b,
        packed_projection_weight_back,
        output_projection_weight_back,
        expansion_weight_back,
        w_down_b,
    ) = again
    out_total = row_total(cotangent)
    grad_proj_w = outer_sum(att_tokens, cotangent)
    grad_down_w = outer_sum(activ, cotangent)
    grad_att_tokens = jnp.einsum(
        "kcw,xw->kcx", cotangent, output_projection_weight_back, preferred_element_type=jnp.float32
    ).astype(jnp.bfloat16)
    grad_activ = jnp.einsum("sle,fe->slf", cotangent, w_down_b, preferred_element_type=jnp.float32)
    expansion_gradient = (grad_activ * gelu_slope(up_pre)).astype(jnp.bfloat16)
    grad_up_w = outer_sum(in_mlp, expansion_gradient)
    grad_up_b = row_total(expansion_gradient)
    perceptron_input_gradient = jnp.einsum(
        "cih,rh->cir", expansion_gradient, expansion_weight_back, preferred_element_type=jnp.float32
    )
    grad_heads = lax.all_to_all(
        grad_att_tokens.reshape(seqs_here, local_len, groups, heads_local * HEAD_DIM),
        "seq",
        split_axis=2,
        concat_axis=1,
        tiled=True,
    )
    grad_heads = grad_heads.reshape(seqs_here, full_len, heads_local, HEAD_DIM)
    grad_packed = lax.map(attend_back, (head_rows, grad_heads, log_sums))
    grad_turned = lax.all_to_all(
        as_sent(grad_packed.reshape(seqs_here, full_len, 1, heads_local * 3 * HEAD_DIM)),
        "seq",
        split_axis=1,
        concat_axis=2,
        tiled=True,
    )
    grad_turned = grad_turned.reshape(seqs_here, local_len, HEADS, 3, HEAD_DIM).astype(jnp.float32)
    packed_projection_gradient = (
        apply_turn(grad_turned, cosine, sine, turn_back, ROT_DIM)
        .astype(jnp.bfloat16)
        .reshape(seqs_here, local_len, 3 * width)
    )
    grad_qkv_w = outer_sum(in_attn, packed_projection_gradient)
    grad_qkv_b = row_total(packed_projection_gradient)
    attention_input_gradient = jnp.einsum(
        "kcw,xw->kcx",
        packed_projection_gradient,
        packed_projection_weight_back,
        preferred_element_type=jnp.float32,
    )
    grad_attn_gain = jnp.sum(flat_rows(attention_input_gradient * normed), axis=0)
    grad_attn_bias = jnp.sum(flat_rows(attention_input_gradient), axis=0)
    grad_mlp_gain = jnp.sum(flat_rows(perceptron_input_gradient * normed), axis=0)
    grad_mlp_bias = jnp.sum(flat_rows(perceptron_input_gradient), axis=0)
    combined = attention_input_gradient * gain_attn_b + perceptron_input_gradient * gain_mlp_b
    input_grad = (cotangent.astype(jnp.float32) + norm_back(combined, normed, inv_std)).astype(
        jnp.bfloat16
    )
    local_grads = (
        grad_attn_gain,
        grad_attn_bias,
        grad_mlp_gain,
        grad_mlp_bias,
        grad_qkv_w,
        grad_qkv_b,
        grad_proj_w,
        out_total,
        grad_up_w,
        grad_up_b,
        grad_down_w,
        out_total,
    )
    owned = (
        lax.psum_scatter(
            local_grads[0].astype(jnp.bfloat16), "dp", scatter_dimension=0, tiled=True
        ).astype(jnp.float32),
        lax.psum_scatter(
            local_grads[1].astype(jnp.bfloat16), "dp", scatter_dimension=0, tiled=True
        ).astype(jnp.float32),
        lax.psum_scatter(
            local_grads[2].astype(jnp.bfloat16), "dp", scatter_dimension=0, tiled=True
        ).astype(jnp.float32),
        lax.psum_scatter(
            local_grads[3].astype(jnp.bfloat16), "dp", scatter_dimension=0, tiled=True
        ).astype(jnp.float32),
        lax.psum_scatter(
            local_grads[4].astype(jnp.bfloat16), "dp", scatter_dimension=0, tiled=True
        ).astype(jnp.float32),
        lax.psum_scatter(
            local_grads[5].astype(jnp.bfloat16), "dp", scatter_dimension=0, tiled=True
        ).astype(jnp.float32),
        lax.psum_scatter(
            local_grads[6].astype(jnp.bfloat16), "dp", scatter_dimension=0, tiled=True
        ).astype(jnp.float32),
        lax.psum_scatter(
            local_grads[7].astype(jnp.bfloat16), "dp", scatter_dimension=0, tiled=True
        ).astype(jnp.float32),
        lax.psum_scatter(
            local_grads[8].astype(jnp.bfloat16), "dp", scatter_dimension=0, tiled=True
        ).astype(jnp.float32),
        lax.psum_scatter(
            local_grads[9].astype(jnp.bfloat16), "dp", scatter_dimension=0, tiled=True
        ).astype(jnp.float32),
        lax.psum_scatter(
            local_grads[10].astype(jnp.bfloat16), "dp", scatter_dimension=0, tiled=True
        ).astype(jnp.float32),
        lax.psum_scatter(
            local_grads[11].astype(jnp.bfloat16), "dp", scatter_dimension=0, tiled=True
        ).astype(jnp.float32),
    )
    owned = (
        lax.psum(owned[0].astype(jnp.bfloat16), "seq").astype(jnp.float32),
        lax.psum(owned[1].astype(jnp.bfloat16), "seq").astype(jnp.float32),
        lax.psum(owned[2].astype(jnp.bfloat16), "seq").astype(jnp.float32),
        lax.psum(owned[3].astype(jnp.bfloat16), "seq").astype(jnp.float32),
        lax.psum(owned[4].astype(jnp.bfloat16), "seq").astype(jnp.float32),
        lax.psum(owned[5].astype(jnp.bfloat16), "seq").astype(jnp.float32),
        lax.psum(owned[6].astype(jnp.bfloat16), "seq").astype(jnp.float32),
        lax.psum(owned[7].astype(jnp.bfloat16), "seq").astype(jnp.float32),
        lax.psum(owned[8].astype(jnp.bfloat16), "seq").astype(jnp.float32),
        lax.psum(owned[9].astype(jnp.bfloat16), "seq").astype(jnp.float32),
        lax.psum(owned[10].astype(jnp.bfloat16), "seq").astype(jnp.float32),
        lax.psum(owned[11].astype(jnp.bfloat16), "seq").astype(jnp.float32),
    )
    return (block_out, input_grad) + tuple(owned)


def solution(mesh):
    in_specs = (
        P("dp", "seq", None),
        P("dp", "seq", None),
        P("dp"),
        P("dp"),
        P("dp"),
        P("dp"),
        P("dp", None),
        P("dp"),
        P("dp", None),
        P("dp"),
        P("dp", None),
        P("dp"),
        P("dp", None),
        P("dp"),
    )
    out_specs = (
        P("dp", "seq", None),
        P("dp", "seq", None),
        P("dp"),
        P("dp"),
        P("dp"),
        P("dp"),
        P("dp", None),
        P("dp"),
        P("dp", None),
        P("dp"),
        P("dp", None),
        P("dp"),
        P("dp", None),
        P("dp"),
    )
    return jax.shard_map(local, mesh=mesh, in_specs=in_specs, out_specs=out_specs, check_vma=False)
```

profile of v0, /device:TPU:1, one launch (start us, length us, event | category | flops | bytes accessed | tf_op | source)
XLA Modules:
  0.0 1370.4 jit_solution(15631571224219352740)
XLA Ops:
  10.0 1.3 fusion.98
  13.3 0.8 dynamic-update-slice.12
  17.5 0.8 dynamic-update-slice.18
  18.4 134.7 %all-reduce.18 = (bf16[3072]{0:T(1024)(128)(2,1)}, bf16[768]{0:T(1024)(128)(2,1)}, bf16[768]{0:T(1024)(128)(2,1)}, bf16[2304]{0:T(1024)(128)(2,1)S(1)}, bf16[768...) all-reduce(bf16[3072]{0:T(1024)(128)(2,1)S(1)} %dynamic-update-slice.18, ...), channel_id=1, replica_groups=mesh['dp'=32,'seq'=4] {'dp'}, use_global_device_ids=true, to_apply=%add.8 | all-reduce | flops 8448 | bytes 33792
  153.1 1.1 convert_reduce_fusion
  154.2 1.2 fusion.77
  155.7 1.9 convolution_convert_fusion.4
  157.6 0.9 copy.131
  158.5 30.5 %all-to-all-start.2 = ((bf16[1,256,4,192]{1,3,0,2:T(8,128)(2,1)}), bf16[1,256,4,192]{1,3,0,2:T(8,128)(2,1)S(1)}, u32[]{:S(2)}, u32[]{:S(2)}) async-start(bf16[1,256,4,192]{1,3,0,2:T(8,128)(2,1)} %bitcast.26), calls=%async_computation.2 | async-start | bytes 786432 | tf_op jit(solution)/shard_map/all_to_all | solution.py:299
  189.0 114.3 %all-gather.5.cloned.1.call-done = bf16[768,2304]{1,0:T(8,128)(2,1)} async-done(((bf16[24,2304]{1,0:T(8,128)(2,1)}), bf16[768,2304]{1,0:T(8,128)(2,1)}) %all-gather.5.cloned.1.call-update) | async-done | bytes 3538960 | tf_op jit(solution)/shard_map/all_gather | solution.py:213
  303.3 4.6 convolution_add_fusion
  307.9 2.0 copy.118
  310.3 1.1 pad_maximum_fusion
  311.5 24.9 %all-to-all-start = ((bf16[1,256,4,576]{1,3,0,2:T(8,128)(2,1)}), bf16[1,256,4,576]{1,3,0,2:T(8,128)(2,1)S(1)}, u32[]{:S(2)}, u32[]{:S(2)}) async-start(bf16[1,256,4,576]{1,3,0,2:T(8,128)(2,1)} %bitcast.5), calls=%async_computation | async-start | bytes 2359296 | tf_op jit(solution)/shard_map/all_to_all | solution.py:253
  337.2 1.2 iota_compare_fusion
  340.4 31.5 %all-to-all-done = bf16[1,256,4,576]{1,3,0,2:T(8,128)(2,1)S(1)} async-done(((bf16[1,256,4,576]{1,3,0,2:T(8,128)(2,1)}), bf16[1,256,4,576]{1,3,0,2:T(8,128)(2,1)S(1)}, u32[]{:S(2)}, u32[]{:S(2)}) %all-to-all-start) | async-done | bytes 1179680 | tf_op jit(solution)/shard_map/all_to_all | solution.py:253
  371.9 0.9 copy.120
  372.8 2.2 squeeze.33
  375.0 2.0 fusion.100
  377.5 1.4 fusion.99
  379.0 1.5 fusion
  381.7 0.9 multiply_convert_fusion.1
  383.0 1.9 multiply_reduce_fusion
  384.9 1.4 multiply_convert_fusion
  386.3 1.1 fusion.56
  389.3 1.2 fusion.44
  390.6 1.2 copy.138
  391.8 6.3 copy.139
  398.7 11.0 reduce.26
  409.7 4.2 reshape.728
  413.8 46.5 %all_to_all.54 = bf16[4,2,73728]{2,1,0:T(2,128)(2,1)} all-to-all(bf16[4,2,73728]{2,1,0:T(2,128)(2,1)} %reshape.728), channel_id=1, replica_groups=mesh['dp'=32,'seq'=4] {'seq'}, dimensions={0} | all-to-all | bytes 2359296 | tf_op jit(solution)/shard_map/all_to_all | solution.py:308
  460.4 4.7 reshape.729
  465.1 6.0 copy.140
  471.1 3.5 reshape.678
  474.6 2.1 copy.141
  477.1 1.0 fusion.95
  478.1 1.0 copy-done.4
  479.2 3.1 convolution_convert_fusion.2
  483.6 1.3 convert_element_type.267
  484.9 11.1 fusion.5
  496.0 132.5 %all-gather.11.cloned.1.call-done = bf16[3072,768]{1,0:T(8,128)(2,1)} async-done(((bf16[96,768]{1,0:T(8,128)(2,1)}), bf16[3072,768]{1,0:T(8,128)(2,1)}) %all-gather.11.cloned.1.call-update) | async-done | bytes 4718608 | tf_op jit(solution)/shard_map/all_gather | solution.py:219
  628.5 5.9 fusion.101
  634.4 1.1 copy-done.9
  635.5 3.7 convolution_convert_fusion.1
  639.5 5.1 convolution_convert_fusion
  644.7 1.6 fusion.54
  646.3 4.3 fusion.55
  651.5 4.0 reduce.27
  656.1 36.4 %all_to_all.55 = bf16[4,2,24576]{2,1,0:T(2,128)(2,1)S(1)} all-to-all(bf16[4,2,24576]{2,1,0:T(2,128)(2,1)S(1)} %reshape.726), channel_id=1, replica_groups=mesh['dp'=32,'seq'=4] {'seq'}, dimensions={0} | all-to-all | bytes 786432 | tf_op jit(solution)/shard_map/all_to_all | solution.py:257
  694.3 1.5 convolution_convert_fusion.3
  698.9 3.3 fusion.102
  702.2 3.9 fusion.94
  706.5 132.6 %all-reduce.17 = (bf16[768]{0:T(1024)(128)(2,1)S(1)}, bf16[768]{0:T(1024)(128)(2,1)S(1)}, bf16[768]{0:T(1024)(128)(2,1)S(1)}, bf16[768]{0:T(1024)(128)(2,1)S(1)}...) all-reduce(bf16[768]{0:T(1024)(128)(2,1)S(1)} %dynamic-update-slice, ...), channel_id=1, replica_groups=mesh['dp'=32,'seq'=4] {'dp'}, use_global_device_ids=true, to_apply=%add.9 | all-reduce | flops 10752 | bytes 43008
  839.1 5.2 fusion.38
  844.3 119.2 %reduce-scatter.9.cloned.1.call-done = bf16[24,3072]{1,0:T(8,128)(2,1)} async-done(((bf16[768,3072]{1,0:T(8,128)(2,1)}), bf16[24,3072]{1,0:T(8,128)(2,1)}) %reduce-scatter.9.cloned.1.call-update) | async-done | bytes 147472 | tf_op jit(solution)/shard_map/reduce_scatter | solution.py:376
  963.5 169.6 %reduce-scatter.11.cloned.1.call-done = bf16[96,768]{1,0:T(8,128)(2,1)} async-done(((bf16[3072,768]{1,0:T(8,128)(2,1)}), bf16[96,768]{1,0:T(8,128)(2,1)}) %reduce-scatter.11.cloned.1.call-update) | async-done | bytes 147472 | tf_op jit(solution)/shard_map/reduce_scatter | solution.py:382
  1133.2 1.1 fusion.74
  1134.8 2.4 fusion.39
  1137.2 154.7 %reduce-scatter.7.cloned.1.call-done = bf16[24,768]{1,0:T(8,128)(2,1)} async-done(((bf16[768,768]{1,0:T(8,128)(2,1)}), bf16[24,768]{1,0:T(8,128)(2,1)}) %reduce-scatter.7.cloned.1.call-update) | async-done | bytes 36880 | tf_op jit(solution)/shard_map/reduce_scatter | solution.py:370
  1291.9 39.4 %all-reduce.19 = (bf16[24]{0:T(256)(128)(2,1)S(1)}, bf16[24]{0:T(256)(128)(2,1)S(1)}, bf16[24]{0:T(256)(128)(2,1)S(1)}, bf16[24]{0:T(256)(128)(2,1)S(1)}, bf16[7...) all-reduce(bf16[24]{0:T(256)(128)(2,1)S(1)} %dynamic-slice.41, ...), channel_id=1, replica_groups=mesh['dp'=32,'seq'=4] {'seq'}, use_global_device_ids=true, to_apply=%region_12.13 | all-reduce | flops 18720 | bytes 74880 | tf_op jit(solution)/shard_map/psum | solution.py:390
  1335.1 22.9 %all-reduce.23.cloned.1.call-done = (bf16[24,2304]{1,0:T(8,128)(2,1)}, bf16[24,3072]{1,0:T(8,128)(2,1)}, bf16[96,768]{1,0:T(8,128)(2,1)}) async-done(((bf16[24,2304]{1,0:T(8,128)(2,1)}, bf16[24,3072]{1,0:T(8,128)(2,1)}, bf16[96,768]{1,0:T(8,128)(2,1)}), (bf16[24,2304]{1,0:T(8,128)(2,1)}, bf16[24,3072]{1,0:T(8,128)(2,1)}, bf16[96,768]{1,0:T(8,128)(2,1)})) %all-reduce.23.cloned.1.call-update) | async-done | bytes 405520 | tf_op jit(solution)/shard_map/psum | solution.py:394
  1358.0 1.6 convert_element_type.301
  1359.6 1.6 convert_element_type.304
  1361.2 1.6 convert_element_type.295
  (176 shorter events, 25.3 us)
Async XLA Ops:
  7.2 296.1 %copy-start.1 = (bf16[1,256,768]{2,1,0:T(8,128)(2,1)S(1)}, bf16[1,256,768]{2,1,0:T(8,128)(2,1)}, u32[]{:S(2)}) copy-start(bf16[1,256,768]{2,1,0:T(8,128)(2,1)} %param.26) | copy-start | bytes 1179652
  7.2 148.5 %all-gather.7.cloned.1.call-start = ((), (), s32[]{:S(2)}) async-start(), calls=%async_computation.9 | async-start | bytes 1216512 | tf_op jit(solution)/shard_map/all_gather | solution.py:215
  7.9 295.4 %all-gather.5.cloned.1.call-start = ((), (), s32[]{:S(2)}) async-start(), calls=%async_computation.8 | async-start | bytes 3649536 | tf_op jit(solution)/shard_map/all_gather | solution.py:213
  8.7 476.2 %all-gather.9.cloned.1.call-start = ((), (), s32[]{:S(2)}) async-start(), calls=%async_computation.10 | async-start | bytes 4866048 | tf_op jit(solution)/shard_map/all_gather | solution.py:217
  9.4 619.1 %all-gather.11.cloned.1.call-start = ((), (), s32[]{:S(2)}) async-start(), calls=%async_computation.11 | async-start | bytes 4866048 | tf_op jit(solution)/shard_map/all_gather | solution.py:219
  153.1 154.8 %copy-start.14 = (f32[768]{0:T(1024)}, f32[768]{0:T(1024)S(1)}, u32[]{:S(2)}) copy-start(f32[768]{0:T(1024)S(1)} %convert_element_type.255) | copy-start | bytes 9220
  153.1 154.8 %copy-start.17 = (f32[768]{0:T(1024)}, f32[768]{0:T(1024)S(1)}, u32[]{:S(2)}) copy-start(f32[768]{0:T(1024)S(1)} %convert_element_type.256) | copy-start | bytes 9220
  154.2 153.7 %copy-start.19 = (f32[256]{0:T(256)}, f32[256]{0:T(256)S(1)}, u32[]{:S(2)}) copy-start(f32[256]{0:T(256)S(1)} %broadcast_multiply_fusion.3) | copy-start | bytes 3076
  155.5 152.4 %copy-start.22 = (f32[256]{0:T(256)}, f32[256]{0:T(256)S(1)}, u32[]{:S(2)}) copy-start(f32[256]{0:T(256)S(1)} %add_rsqrt_fusion) | copy-start | bytes 3076
  155.7 154.4 %copy-start.12 = (f32[256,16]{0,1:T(8,128)}, f32[256,16]{0,1:T(8,128)S(1)}, u32[]{:S(2)}) copy-start(f32[256,16]{0,1:T(8,128)S(1)} %get-tuple-element.167) | copy-start | bytes 49156
  158.5 153.0 %all-to-all-start.2 = ((bf16[1,256,4,192]{1,3,0,2:T(8,128)(2,1)}), bf16[1,256,4,192]{1,3,0,2:T(8,128)(2,1)S(1)}, u32[]{:S(2)}, u32[]{:S(2)}) async-start(bf16[1,256,4,192]{1,3,0,2:T(8,128)(2,1)} %bitcast.26), calls=%async_computation.2 | async-start | bytes 786432 | tf_op jit(solution)/shard_map/all_to_all | solution.py:299
  311.5 60.4 %all-to-all-start = ((bf16[1,256,4,576]{1,3,0,2:T(8,128)(2,1)}), bf16[1,256,4,576]{1,3,0,2:T(8,128)(2,1)S(1)}, u32[]{:S(2)}, u32[]{:S(2)}) async-start(bf16[1,256,4,576]{1,3,0,2:T(8,128)(2,1)} %bitcast.5), calls=%async_computation | async-start | bytes 2359296 | tf_op jit(solution)/shard_map/all_to_all | solution.py:253
  336.4 507.9 %reduce-scatter.5.cloned.1.call-start = ((), (), s32[]{:S(2)}) async-start(), calls=%async_computation.12 | async-start | bytes 3649536 | tf_op jit(solution)/shard_map/reduce_scatter | solution.py:364
  375.0 2.5 copy-start.3
  375.0 2.5 copy-start.11
  377.1 1.9 copy-start.26
  377.5 1.5 copy-start.27
  379.0 1.5 copy-start.28
  379.0 10.3 copy-start
  379.0 1.6 copy-start.7
  380.6 1.1 copy-start.30
  381.7 1.3 copy-start.8
  474.6 2.3 copy-start.13
  476.8 2.3 copy-start.15
  476.8 2.3 copy-start.18
  476.9 2.3 copy-start.20
  476.9 2.3 copy-start.23
  478.1 1.0 copy-start.4
  482.3 0.6 copy-start.33
  482.3 2.6 copy-start.21
  482.3 2.6 copy-start.24
  482.3 481.2 %reduce-scatter.9.cloned.1.call-start = ((), (), s32[]{:S(2)}) async-start(), calls=%async_computation.14 | async-start | bytes 4866048 | tf_op jit(solution)/shard_map/reduce_scatter | solution.py:376
  634.4 1.1 copy-start.9
  639.2 493.9 %reduce-scatter.11.cloned.1.call-start = ((), (), s32[]{:S(2)}) async-start(), calls=%async_computation.15 | async-start | bytes 4866048 | tf_op jit(solution)/shard_map/reduce_scatter | solution.py:382
  644.6 647.3 %reduce-scatter.7.cloned.1.call-start = ((), (), s32[]{:S(2)}) async-start(), calls=%async_computation.13 | async-start | bytes 1216512 | tf_op jit(solution)/shard_map/reduce_scatter | solution.py:370
  644.7 1.6 copy-start.29
  644.7 1.6 copy-start.31
  655.5 38.8 %copy-start.2 = (bf16[1,256,768]{2,1,0:T(8,128)(2,1)S(1)}, bf16[1,256,768]{2,1,0:T(8,128)(2,1)}, u32[]{:S(2)}) copy-start(bf16[1,256,768]{2,1,0:T(8,128)(2,1)} %param.27) | copy-start | bytes 1179652
  693.3 5.0 copy-start.34
  693.3 5.2 copy-start.35
  693.3 5.4 copy-start.25
  693.3 5.5 copy-start.5
  695.9 662.1 %all-reduce.23.cloned.1.call-start = ((), (), s32[]{:S(2)}) async-start(), calls=%async_computation.16 | async-start | bytes 811008 | tf_op jit(solution)/shard_map/psum | solution.py:394
  698.8 3.3 copy-start.10
  698.9 3.3 copy-start.16
  702.2 4.3 copy-start.32
  839.1 295.7 %copy-start.6 = (bf16[768,768]{1,0:T(8,128)(2,1)S(1)}, bf16[768,768]{1,0:T(8,128)(2,1)}, u32[]{:S(2)}) copy-start(bf16[768,768]{1,0:T(8,128)(2,1)} %all-gather.7.cloned.1.call-done) | copy-start | bytes 3538948
  1332.0 31.4 %copy-start.36 = (f32[24]{0:T(128)}, f32[24]{0:T(128)S(1)}, u32[]{:S(2)}) copy-start(f32[24]{0:T(128)S(1)} %convert_element_type.299) | copy-start | bytes 292
Sparse Core Ops, SparseCore 0:
  9.7 133.2 all-gather.6
  144.6 158.6 all-gather.4
  305.0 167.5 all-gather.8
  474.1 154.3 all-gather.10
  630.7 164.0 reduce-scatter.4
  797.3 166.2 reduce-scatter.8
  966.0 167.0 reduce-scatter.10
  1135.6 156.1 reduce-scatter.6
  1294.6 63.3 all-reduce.22
where the time goes:
time: 1380 us; the launch traced here: 1370 us
  waiting for transfers between devices  747 us (54%)
  blocking collectives  390 us (28%)
  matrix products  68.2 us (5%)
  starting transfers between devices  56.3 us (4%)
  local copies, waits for them, and re-layouts  51.2 us (4%)
  other arithmetic  38.6 us (3%)
  between operations  19 us (1%)
    unnamed x2, blocking collectives  267 us
    reduce_scatter x1, waiting for transfers between devices, local(): lax.psum_scatter(local_grads[10].astype(jnp.bfloat16), 'dp', scatter_dime...  170 us
    reduce_scatter x1, waiting for transfers between devices, local(): lax.psum_scatter(local_grads[6].astype(jnp.bfloat16), 'dp', scatter_dimen...  155 us
    all_gather x1, waiting for transfers between devices, local(): lax.all_gather(shards[10], 'dp', axis=0, tiled=True)  133 us
    reduce_scatter x1, waiting for transfers between devices, local(): lax.psum_scatter(local_grads[8].astype(jnp.bfloat16), 'dp', scatter_dimen...  119 us
    all_gather x1, waiting for transfers between devices, local(): lax.all_gather(shards[4], 'dp', axis=0, tiled=True)  114 us
    all_to_all x1, blocking collectives, local(): lax.all_to_all(as_sent(grad_packed.reshape(seqs_here, full_len, 1, heads_...  46.5 us
    psum x1, blocking collectives, local(): lax.psum(owned[0].astype(jnp.bfloat16), 'seq').astype(jnp.float32)  39.4 us
  transfers between devices with their start and end apart: 11, of which 7 were waited for; matrix products, arithmetic and copies ran while one was open for 11% of the time, Pallas kernels for 0%

commit v1 on v0

v1 whole, which is shorter than its diff:
```python
import math

import jax
import jax.numpy as jnp
from jax import lax
from jax.experimental import pallas as pl
from jax.experimental.pallas import tpu as pltpu
from jax.sharding import PartitionSpec as P

HEADS = 12
HEAD_DIM = 64
ROT_DIM = 16
WIDTH = 768
EPSILON = 1e-05
MASKED = -1e30
MESH = pl.DeviceIdType.MESH
BF = jnp.bfloat16
F32 = jnp.float32
MIB = 1 << 20


def coords():
    dp = lax.axis_index("dp")
    seq = lax.axis_index("seq")
    x = lax.div(dp, 8)
    y = lax.rem(lax.div(dp, 2), 4)
    z_lo = lax.rem(dp, 2)
    z_hi = lax.div(seq, 2)
    core = lax.rem(seq, 2)
    return x, y, z_hi * 2 + z_lo, core


def device(x, y, z, core):
    return (x * 8 + y * 2 + lax.rem(z, 2), lax.div(z, 2) * 2 + core)


def around(at, offset):
    return lax.rem(at + offset, 4)


def copy_to(src, dst, send_sem, recv_sem, target):
    return pltpu.make_async_remote_copy(
        src_ref=src,
        dst_ref=dst,
        send_sem=send_sem,
        recv_sem=recv_sem,
        device_id=target,
        device_id_type=MESH,
    )


def dot(left, right):
    return jnp.dot(left, right, preferred_element_type=F32)


def dot_t(left, right):
    return lax.dot_general(left, right, (((1,), (1,)), ((), ())), preferred_element_type=F32)


def dot_a(left, right):
    return lax.dot_general(left, right, (((0,), (0,)), ((), ())), preferred_element_type=F32)


def greet(targets):
    barrier = pltpu.get_barrier_semaphore()
    for target in targets:
        pl.semaphore_signal(barrier, inc=1, device_id=target, device_id_type=MESH)
    pl.semaphore_wait(barrier, len(targets))


def weight_rows(ref):
    value = ref[...]
    return value.reshape(value.shape[0] * value.shape[1] * value.shape[2], value.shape[3])


def slab_rows(value):
    return value.reshape(value.shape[0] * value.shape[1], value.shape[2])


N_GATHER = 13


def front_kernel(
    x_in,
    g_in,
    w_a,
    w_d,
    vec_in,
    tab,
    heads,
    ob_part,
    gim_part,
    grads,
    blocks_out,
    p_other,
    xx,
    gh,
    in_attn,
    in_attn_t,
    vec,
    small,
    late,
    vecs,
    z_a,
    z_v,
    normed,
    in_mlp,
    in_mlp_t,
    send_heads,
    gg,
    pair_ss,
    pair_rs,
    one_ss,
    one_rs,
    two_ss,
    two_rs,
    head_ss,
    head_rs,
):
    x, y, z, core = coords()
    z_lo = lax.rem(z, 2)
    z_hi = lax.div(z, 2)
    x_peers = [device(around(x, o), y, z, core) for o in (1, 2, 3)]
    y_peers = [device(x, around(y, o), z, core) for o in (1, 2, 3)]
    sibling = device(x, y, z, 1 - core)
    z_pair = device(x, y, z_hi * 2 + 1 - z_lo, core)
    z_far = device(x, y, around(z, 2), core)
    greet(x_peers + y_peers + [sibling, z_pair, z_far])

    def block(i):
        return blocks_out.at[i] if i < 4 else late.at[i - 4]

    pair = [
        copy_to(w_a.at[pl.ds(0, 4)], z_a.at[pl.ds(0, 4)], pair_ss.at[0], pair_rs.at[0], z_pair),
        copy_to(vec_in, z_v, pair_ss.at[1], pair_rs.at[1], z_pair),
        copy_to(w_a.at[pl.ds(4, 4)], z_a.at[pl.ds(4, 4)], pair_ss.at[2], pair_rs.at[2], z_pair),
    ]
    for half in range(2):
        pair.append(
            copy_to(
                w_d.at[half],
                late.at[4 + half * 2 + z_lo, x, y],
                pair_ss.at[3 + half],
                pair_rs.at[3 + half],
                z_pair,
            )
        )
    for item in pair:
        item.start()
    tokens = [
        copy_to(x_in, xx.at[core], pair_ss.at[5], pair_rs.at[5], sibling),
        copy_to(g_in, gg.at[core], pair_ss.at[6], pair_rs.at[6], sibling),
    ]
    for item in tokens:
        item.start()
    xx[core] = x_in[...]
    gg[core] = g_in[...]
    for half in range(2):
        late[4 + half * 2 + z_lo, x, y] = w_d[half]

    def assemble(i):
        own = w_a[i].astype(F32)
        other = z_a[i].astype(F32)
        first = z_lo == 0
        both = jnp.concatenate(
            [jnp.where(first, own, other), jnp.where(first, other, own)], axis=0
        ).astype(BF)
        block(i)[x, y] = both

    def gather_ref(i):
        return vecs if i == 12 else block(i)

    def phase(i, number):
        ref = gather_ref(i)
        along_y = (i % 2 == 0) == (number == 1)
        ss, rs = (one_ss, one_rs) if number == 1 else (two_ss, two_rs)
        copies = []
        for k, o in enumerate((1, 2, 3)):
            target = y_peers[k] if along_y else x_peers[k]
            if number == 1:
                part = ref.at[x, y]
            elif along_y:
                part = ref.at[:, y]
            else:
                part = ref.at[x]
            copies.append(copy_to(part, part, ss.at[i, k], rs.at[i, k], target))
        return copies

    def arrivals(i, number):
        ref = gather_ref(i)
        along_y = (i % 2 == 0) == (number == 1)
        ss, rs = (one_ss, one_rs) if number == 1 else (two_ss, two_rs)
        for k, o in enumerate((1, 2, 3)):
            xs = x if along_y else around(x, 4 - o)
            ys = around(y, 4 - o) if along_y else y
            if number == 1:
                part = ref.at[xs, ys]
            elif along_y:
                part = ref.at[:, ys]
            else:
                part = ref.at[xs]
            target = y_peers[k] if along_y else x_peers[k]
            copy_to(part, part, ss.at[i, k], rs.at[i, k], target).wait_recv()

    def start(i, number):
        for item in phase(i, number):
            item.start()

    early_ids = (12, 0, 1, 2, 3)
    late_ids = tuple(range(4, 12))
    pair[0].wait_recv()
    pair[1].wait_recv()
    vecs[x, y] = (vec_in[...].astype(F32) + z_v[...].astype(F32)).astype(BF)
    for i in range(4):
        assemble(i)
    for i in early_ids:
        start(i, 1)
    pair[2].wait_recv()
    pair[3].wait_recv()
    pair[4].wait_recv()
    for i in range(4, 8):
        assemble(i)
    for item in tokens:
        item.wait_recv()

    for half in range(2):

        @pl.loop(0, 2)
        def _(step):
            rows = pl.ds(pl.multiple_of(step * 128, 128), 128)
            out_rows = pl.ds(pl.multiple_of(half * 256 + step * 128, 128), 128)
            values = xx[half, rows, :].astype(F32)
            center = values - jnp.mean(values, axis=-1, keepdims=True)
            inv_std = lax.rsqrt(jnp.mean(center * center, axis=-1, keepdims=True) + EPSILON)
            normed[out_rows, :] = center * inv_std
            cot = gg[half, rows, :]
            gh[0, out_rows, :] = cot[:, :384]
            gh[1, out_rows, :] = cot[:, 384:]

    for i in early_ids:
        arrivals(i, 1)
        start(i, 2)
    for i in late_ids:
        start(i, 1)
    arrivals(12, 2)
    total = jnp.zeros((16, WIDTH), F32)
    for i in range(4):
        for j in range(4):
            total = total + vecs[i, j].astype(F32)
    vec[...] = total

    @pl.loop(0, 4)
    def _(step):
        rows = pl.ds(pl.multiple_of(step * 128, 128), 128)
        values = normed[rows, :]
        in_attn[rows, :] = (values * vec[0:1, :] + vec[1:2, :]).astype(BF)
        in_mlp[rows, :] = (values * vec[2:3, :] + vec[3:4, :]).astype(BF)

    in_attn_t[...] = in_attn[...].T
    in_mlp_t[...] = in_mlp[...].T

    for i in (3, 0, 1, 2):
        arrivals(i, 2)
    swap_p = copy_to(blocks_out.at[3], p_other, pair_ss.at[7], pair_rs.at[7], sibling)
    swap_p.start()
    for i in late_ids:
        arrivals(i, 1)
        start(i, 2)

    cosine = tab[0]
    left_sine = tab[1]
    right_sine = tab[2]
    activations = in_attn[...]
    value_pre = dot(activations, weight_rows(blocks_out.at[2]))
    value_pre = (value_pre + vec[7:8, :384]).astype(BF)
    swap_p.wait_recv()
    for group in range(2):
        far = z_hi != group
        pre = dot(activations, weight_rows(blocks_out.at[group]))
        pre = pre + vec[6:7, group * 384 : group * 384 + 384]
        own_p = slab_rows(blocks_out[3, group * 2 + core])
        other_p = slab_rows(p_other[group * 2 + core])
        grad_att = dot_t(gh[core], own_p) + dot_t(gh[1 - core], other_p)
        grad_att = grad_att.astype(BF)
        for head in range(3):
            part = pre[:, head * 128 : head * 128 + 128]
            turned = (
                part * cosine
                + pltpu.roll(part, 120, 1) * left_sine
                + pltpu.roll(part, 8, 1) * right_sine
            ).astype(BF)
            at = head * 64
            rest = jnp.concatenate(
                [
                    value_pre[:, group * 192 + at : group * 192 + at + 64],
                    grad_att[:, at : at + 64],
                ],
                axis=1,
            )

            @pl.when(far)
            def _():
                send_heads[head, :, 0:128] = turned
                send_heads[head, :, 128:256] = rest

            @pl.when(jnp.logical_not(far))
            def _():
                heads[head, group, :, 0:128] = turned
                heads[head, group, :, 128:256] = rest

    far_copies = [
        copy_to(
            send_heads.at[head], heads.at[head, z_hi], head_ss.at[head], head_rs.at[head], z_far
        )
        for head in range(3)
    ]
    for item in far_copies:
        item.start()

    for i in late_ids:
        arrivals(i, 2)
    ob_part[...] = jnp.zeros((512, WIDTH), F32)
    gim_part[...] = jnp.zeros((512, WIDTH), F32)
    small[...] = jnp.zeros((16, WIDTH), F32)

    @pl.loop(0, 4)
    def _(b):
        weight_up = weight_rows(late.at[b])
        down = [
            jnp.concatenate(
                [slab_rows(late[4 + 2 * half, b]), slab_rows(late[5 + 2 * half, b])], axis=0
            )
            for half in range(2)
        ]
        bias = jnp.where(
            lax.rem(b, 2) == 0,
            jnp.where(b < 2, vec[8:9, :384], vec[9:10, :384]),
            jnp.where(b < 2, vec[8:9, 384:], vec[9:10, 384:]),
        )
        up_pre = dot(in_mlp[...], weight_up) + bias
        cdf = 0.5 * (1.0 + lax.erf(up_pre * (1.0 / math.sqrt(2.0))))
        activ = (up_pre * cdf).astype(BF)
        density = jnp.exp(-0.5 * up_pre * up_pre) * (1.0 / math.sqrt(2.0 * math.pi))
        slope = cdf + up_pre * density
        grad_activ = dot_t(gh[0], down[0]) + dot_t(gh[1], down[1])
        grad_up = grad_activ * slope
        low_grad = grad_up.astype(BF)
        bias_grad = jnp.sum(low_grad.astype(F32), axis=0, keepdims=True)
        for k in range(4):

            @pl.when(b == k)
            def _():
                small[7 + k // 2 : 8 + k // 2, (k % 2) * 384 : (k % 2) * 384 + 384] = bias_grad

        activ_t = activ.T
        for half in range(2):
            ob_part[:, half * 384 : half * 384 + 384] += dot(activ, down[half])
            grad_down = dot(activ_t, gh[half]).astype(BF)
            grads[4 + 2 * half, b] = grad_down[:192].reshape(4, 48, 384)
            grads[5 + 2 * half, b] = grad_down[192:].reshape(4, 48, 384)
        grads[b] = dot(in_mlp_t[...], low_grad).astype(BF).reshape(4, 4, 48, 384)
        gim_part[...] += dot_t(low_grad, weight_up)

    grad_in = gim_part[...]
    small[2:3, :] = jnp.sum(grad_in * normed[...], axis=0, keepdims=True)
    small[3:4, :] = jnp.sum(grad_in, axis=0, keepdims=True)
    small[4:5, :] = jnp.sum(g_in[...].astype(F32), axis=0, keepdims=True)

    for item in far_copies:
        item.wait()
    swap_p.wait_send()
    for item in pair + tokens:
        item.wait_send()
    for i in early_ids + late_ids:
        for number in (1, 2):
            for item in phase(i, number):
                item.wait_send()


def front(x_in, g_in, w_a, w_d, vec_in, tab):
    shape = jax.ShapeDtypeStruct
    outs = (
        shape((3, 2, 512, 256), BF),
        shape((512, WIDTH), F32),
        shape((512, WIDTH), F32),
        shape((8, 4, 4, 48, 384), BF),
        shape((4, 4, 4, 48, 384), BF),
        shape((4, 4, 48, 384), BF),
        shape((2, 256, WIDTH), BF),
        shape((2, 512, 384), BF),
        shape((512, WIDTH), BF),
        shape((WIDTH, 512), BF),
        shape((16, WIDTH), F32),
        shape((16, WIDTH), F32),
    )
    dma = pltpu.SemaphoreType.DMA
    vmem = pl.BlockSpec(memory_space=pltpu.VMEM)
    return pl.pallas_call(
        front_kernel,
        name="front",
        out_shape=outs,
        in_specs=[vmem] * 6,
        out_specs=(vmem,) * len(outs),
        scratch_shapes=[
            pltpu.VMEM((8, 4, 4, 48, 384), BF),
            pltpu.VMEM((4, 4, 16, WIDTH), BF),
            pltpu.VMEM((8, 24, 384), BF),
            pltpu.VMEM((16, WIDTH), BF),
            pltpu.VMEM((512, WIDTH), F32),
            pltpu.VMEM((512, WIDTH), BF),
            pltpu.VMEM((WIDTH, 512), BF),
            pltpu.VMEM((3, 512, 256), BF),
            pltpu.VMEM((2, 256, WIDTH), BF),
            dma((8,)),
            dma((8,)),
            dma((N_GATHER, 3)),
            dma((N_GATHER, 3)),
            dma((N_GATHER, 3)),
            dma((N_GATHER, 3)),
            dma((3,)),
            dma((3,)),
        ],
        compiler_params=pltpu.CompilerParams(
            collective_id=0, has_side_effects=True, vmem_limit_bytes=60 * MIB
        ),
    )(x_in, g_in, w_a, w_d, vec_in, tab)


def back_kernel(
    heads,
    ob_part,
    gim_part,
    mlp_grads,
    weights,
    p_other,
    xx,
    gh,
    in_attn,
    in_attn_t,
    vec,
    small_in,
    tab,
    g_in,
    block_out,
    input_grad,
    owned,
    owned_down,
    small,
    attn_grads,
    own_rows,
    far_rows,
    back_rows,
    dk_acc,
    dv_acc,
    att,
    att_other,
    grad_qk,
    grad_v,
    h_part,
    token_in,
    r_one,
    mid,
    r_two,
    done,
    r_z,
    share,
    small_r,
    one_ss,
    one_rs,
    two_ss,
    two_rs,
    z_ss,
    z_rs,
    head_ss,
    head_rs,
    pair_ss,
    pair_rs,
    small_ss,
    small_rs,
    share_ss,
    share_rs,
):
    x, y, z, core = coords()
    z_lo = lax.rem(z, 2)
    z_hi = lax.div(z, 2)
    x_peers = [device(around(x, o), y, z, core) for o in (1, 2, 3)]
    y_peers = [device(x, around(y, o), z, core) for o in (1, 2, 3)]
    z_peers = [device(x, y, around(z, o), core) for o in (1, 2, 3)]
    z_cross = [device(x, y, around(z, o), 1 - core) for o in (1, 2, 3)]
    sibling = device(x, y, z, 1 - core)
    z_far = z_peers[1]
    greet(x_peers + y_peers + z_peers + z_cross + [sibling])

    def grad_ref(i):
        return attn_grads.at[i] if i < 4 else mlp_grads.at[i - 4]

    def first_copies(i):
        ref = grad_ref(i)
        copies = []
        for k, o in enumerate((1, 2, 3)):
            if i % 2 == 0:
                part, target = ref.at[around(x, o)], x_peers[k]
            else:
                part, target = ref.at[:, around(y, o)], y_peers[k]
            copies.append(copy_to(part, r_one.at[i, k], one_ss.at[i, k], one_rs.at[i, k], target))
        return copies

    def second_copies(i):
        copies = []
        for k, o in enumerate((1, 2, 3)):
            if i % 2 == 0:
                part, target = mid.at[i, around(y, o)], y_peers[k]
            else:
                part, target = mid.at[i, around(x, o)], x_peers[k]
            copies.append(copy_to(part, r_two.at[i, k], two_ss.at[i, k], two_rs.at[i, k], target))
        return copies

    def third_copies(group):
        return [
            copy_to(
                done.at[group * 4 + around(z, o)],
                r_z.at[group, k],
                z_ss.at[group, k],
                z_rs.at[group, k],
                z_peers[k],
            )
            for k, o in enumerate((1, 2, 3))
        ]

    def first_sum(i):
        for item in first_copies(i):
            item.wait_recv()
        ref = grad_ref(i)

        @pl.loop(0, 4)
        def _(j):
            own = ref[x, j] if i % 2 == 0 else ref[j, y]
            total = own.astype(F32)
            for k in range(3):
                total = total + r_one[i, k, j].astype(F32)
            mid[i, j] = total.astype(BF)

    def second_sum(i):
        for item in second_copies(i):
            item.wait_recv()
        total = mid[i, y if i % 2 == 0 else x].astype(F32)
        for k in range(3):
            total = total + r_two[i, k].astype(F32)
        done[i] = total.astype(BF)

    def third_sum(group):
        for item in third_copies(group):
            item.wait_recv()
        total = done[group * 4 + z].astype(F32)
        for k in range(3):
            total = total + r_z[group, k].astype(F32)
        return total

    def start(copies):
        for item in copies:
            item.start()

    mlp_ids = tuple(range(4, 12))
    attn_ids = tuple(range(4))
    for i in mlp_ids:
        start(first_copies(i))

    scale = 1.0 / math.sqrt(HEAD_DIM)

    def far_copy(head):
        return copy_to(
            far_rows.at[head],
            back_rows.at[head],
            head_ss.at[head],
            head_rs.at[head],
            z_far,
        )

    @pl.loop(0, 3)
    def _(head):
        packed = heads[head].reshape(1024, 256)
        queries = packed[:, 0:64]
        key_rows = packed[:, 64:128]
        value_rows = packed[:, 128:192]
        grad_rows = packed[:, 192:256]
        dk_acc[...] = jnp.zeros((1024, HEAD_DIM), F32)
        dv_acc[...] = jnp.zeros((1024, HEAD_DIM), F32)
        dq_parts = []
        out_parts = []
        for blk in range(4):
            lo, hi = blk * 256, blk * 256 + 256
            q = queries[lo:hi]
            do = grad_rows[lo:hi]
            scores = dot_t(q, key_rows[:hi]) * scale
            row_place = lax.broadcasted_iota(jnp.int32, (256, hi), 0) + lo
            col_place = lax.broadcasted_iota(jnp.int32, (256, hi), 1)
            scores = jnp.where(row_place >= col_place, scores, MASKED)
            peak = jnp.max(scores, axis=-1, keepdims=True)
            expo = jnp.exp(scores - peak)
            probs = expo * (1.0 / jnp.sum(expo, axis=-1, keepdims=True))
            low_probs = probs.astype(BF)
            out_parts.append(dot(low_probs, value_rows[:hi]).astype(BF))
            grad_probs = dot_t(do, value_rows[:hi])
            inner = jnp.sum(probs * grad_probs, axis=-1, keepdims=True)
            grad_scores = (probs * (grad_probs - inner)).astype(BF)
            dq_parts.append((dot(grad_scores, key_rows[:hi]) * scale).astype(BF))
            dk_acc[:hi, :] += dot_a(grad_scores, q)
            dv_acc[:hi, :] += dot_a(low_probs, do)
        dk = (dk_acc[...] * scale).astype(BF)
        dv = dv_acc[...].astype(BF)
        dq = jnp.concatenate(dq_parts, axis=0)
        out = jnp.concatenate(out_parts, axis=0)
        result = jnp.concatenate([dq, dk, dv, out], axis=1)
        near = z_hi == 0
        own_rows[head] = jnp.where(near, result[:512], result[512:])
        far_rows[head] = jnp.where(near, result[512:], result[:512])
        far_copy(head).start()

    for i in mlp_ids:
        first_sum(i)
        start(second_copies(i))
    for i in mlp_ids:
        second_sum(i)
    start(third_copies(1))
    start(third_copies(2))

    for head in range(3):
        far_copy(head).wait_recv()
    cosine = tab[0]
    left_sine = tab[1]
    right_sine = tab[2]
    for group in range(2):
        mine = z_hi == group
        for head in range(3):
            rows = jnp.where(mine, own_rows[head], back_rows[head])
            part = rows[:, 0:128].astype(F32)
            turned = (
                part * cosine
                - pltpu.roll(part, 120, 1) * left_sine
                - pltpu.roll(part, 8, 1) * right_sine
            ).astype(BF)
            grad_qk[group, :, head * 128 : head * 128 + 128] = turned
            grad_v[:, group * 192 + head * 64 : group * 192 + head * 64 + 64] = rows[:, 128:192]
            att[group, :, head * 64 : head * 64 + 64] = rows[:, 192:256]
    swap_att = copy_to(att, att_other, pair_ss.at[0], pair_rs.at[0], sibling)
    swap_att.start()

    for group in range(2):
        attn_grads[group] = dot(in_attn_t[...], grad_qk[group]).astype(BF).reshape(4, 4, 48, 384)
        start(first_copies(group))
    attn_grads[2] = dot(in_attn_t[...], grad_v[...]).astype(BF).reshape(4, 4, 48, 384)
    start(first_copies(2))
    swap_att.wait_recv()
    for group in range(2):
        attn_grads[3, group * 2 + core] = (
            dot_a(att[group], gh[core]).astype(BF).reshape(4, 48, 384)
        )
        attn_grads[3, group * 2 + 1 - core] = (
            dot_a(att_other[group], gh[core]).astype(BF).reshape(4, 48, 384)
        )
    start(first_copies(3))

    small[...] = small_in[...]
    for group in range(2):
        small[5:6, group * 384 : group * 384 + 384] = jnp.sum(
            grad_qk[group].astype(F32), axis=0, keepdims=True
        )
    small[6:7, :384] = jnp.sum(grad_v[...].astype(F32), axis=0, keepdims=True)
    grad_in = (
        dot_t(grad_qk[0], weight_rows(weights.at[0]))
        + dot_t(grad_qk[1], weight_rows(weights.at[1]))
        + dot_t(grad_v[...], weight_rows(weights.at[2]))
    )
    h_part[...] = grad_in * vec[0:1, :] + gim_part[...] * vec[2:3, :]
    small[1:2, :] = jnp.sum(grad_in, axis=0, keepdims=True)
    gain_grad = jnp.zeros((1, WIDTH), F32)
    for half in range(2):
        values = xx[half].astype(F32)
        center = values - jnp.mean(values, axis=-1, keepdims=True)
        inv_std = lax.rsqrt(jnp.mean(center * center, axis=-1, keepdims=True) + EPSILON)
        gain_grad = gain_grad + jnp.sum(
            grad_in[half * 256 : half * 256 + 256] * (center * inv_std), axis=0, keepdims=True
        )
    small[0:1, :] = gain_grad

    def small_copies(number):
        peers = (x_peers, y_peers, z_peers)[number]
        return [
            copy_to(
                small_r.at[9 + number],
                small_r.at[number * 3 + k],
                small_ss.at[number, k],
                small_rs.at[number, k],
                peers[k],
            )
            for k in range(3)
        ]

    def small_sum(number):
        total = small_r[9 + number]
        for k, item in enumerate(small_copies(number)):
            item.wait_recv()
            total = total + small_r[number * 3 + k]
        return total

    small_r[9] = small[...]
    start(small_copies(0))

    other_rows = pl.ds(pl.multiple_of((1 - core) * 256, 256), 256)
    my_rows = pl.ds(pl.multiple_of(core * 256, 256), 256)
    swap_h = copy_to(
        h_part.at[other_rows], token_in.at[0], pair_ss.at[1], pair_rs.at[1], sibling
    )
    swap_h.start()
    for group in range(2):
        own_p = slab_rows(weights[3, group * 2 + core])
        other_p = slab_rows(p_other[group * 2 + core])
        left = att[group]
        for half in range(2):
            cols = slice(half * 384, half * 384 + 384)
            matrix = jnp.where(core == half, own_p, other_p)
            ob_part[:, cols] += dot(left, matrix)
    swap_ob = copy_to(
        ob_part.at[other_rows], token_in.at[1], pair_ss.at[2], pair_rs.at[2], sibling
    )
    swap_ob.start()

    for i in attn_ids:
        first_sum(i)
        start(second_copies(i))
    small_r[10] = small_sum(0)
    start(small_copies(1))

    swap_h.wait_recv()
    swap_ob.wait_recv()
    values = xx[core].astype(F32)
    center = values - jnp.mean(values, axis=-1, keepdims=True)
    inv_std = lax.rsqrt(jnp.mean(center * center, axis=-1, keepdims=True) + EPSILON)
    norm_rows = center * inv_std
    grad_norm = h_part[my_rows, :] + token_in[0]
    input_grad[...] = (
        g_in[...].astype(F32)
        + inv_std
        * (
            grad_norm
            - jnp.mean(grad_norm, axis=-1, keepdims=True)
            - norm_rows * jnp.mean(grad_norm * norm_rows, axis=-1, keepdims=True)
        )
    ).astype(BF)
    block_out[...] = (
        values + ob_part[my_rows, :] + token_in[1] + (vec[4:5, :] + vec[5:6, :])
    ).astype(BF)

    for i in attn_ids:
        second_sum(i)
    start(third_copies(0))
    small_r[11] = small_sum(1)
    start(small_copies(2))

    def split_rows(group, total):
        share[0, group] = total[:24].astype(BF)
        share[1, group] = total[24:].astype(BF)

    split_rows(1, third_sum(1))
    down_total = third_sum(2).astype(BF)
    owned_down[core, z_hi] = down_total
    split_rows(0, third_sum(0))
    owned[core, z] = share[z_lo]

    peers = []
    for k, o in enumerate((1, 2, 3)):
        peers.append((z_peers[k], around(z, o), around(z, 4 - o), core, k))
        peers.append((z_cross[k], around(z, o), around(z, 4 - o), 1 - core, 3 + k))
    peers.append((sibling, z, z, 1 - core, 6))
    share_copies = []
    share_waits = []
    for target, z_to, z_from, core_from, k in peers:
        share_copies.append(
            copy_to(
                share.at[lax.rem(z_to, 2)],
                owned.at[core, z],
                share_ss.at[k],
                share_rs.at[k],
                target,
            )
        )
        share_waits.append(
            copy_to(
                share.at[0],
                owned.at[core_from, z_from],
                share_ss.at[k],
                share_rs.at[k],
                target,
            )
        )
    for target, core_from, hi_from, k in (
        (z_peers[1], core, 1 - z_hi, 7),
        (z_cross[1], 1 - core, 1 - z_hi, 8),
        (sibling, 1 - core, z_hi, 9),
    ):
        share_copies.append(
            copy_to(
                owned_down.at[core, z_hi],
                owned_down.at[core, z_hi],
                share_ss.at[k],
                share_rs.at[k],
                target,
            )
        )
        share_waits.append(
            copy_to(
                owned_down.at[core_from, hi_from],
                owned_down.at[core_from, hi_from],
                share_ss.at[k],
                share_rs.at[k],
                target,
            )
        )
    start(share_copies)
    small_r[12] = small_sum(2)
    swap_small = copy_to(
        small_r.at[12], small_r.at[13], pair_ss.at[3], pair_rs.at[3], sibling
    )
    swap_small.start()
    swap_small.wait_recv()
    small[...] = jnp.zeros((16, WIDTH), F32)
    small[0:8, :] = small_r[12, 0:8, :] + small_r[13, 0:8, :]
    for row in range(4):
        low = jnp.where(core == 0, small_r[12, 5 + row : 6 + row, :], small_r[13, 5 + row : 6 + row, :])
        high = jnp.where(core == 0, small_r[13, 5 + row : 6 + row, :], small_r[12, 5 + row : 6 + row, :])
        small[5 + row : 6 + row, :] = low
        small[9 + row : 10 + row, :] = high

    for item in share_waits:
        item.wait_recv()
    for item in share_copies + [swap_att, swap_h, swap_ob, swap_small]:
        item.wait_send()
    for head in range(3):
        far_copy(head).wait_send()
    for i in attn_ids + mlp_ids:
        for item in first_copies(i) + second_copies(i):
            item.wait_send()
    for group in range(3):
        for item in third_copies(group):
            item.wait_send()
    for number in range(3):
        for item in small_copies(number):
            item.wait_send()


def back(heads, ob_part, gim_part, mlp_grads, weights, p_other, xx, gh, in_attn, in_attn_t, vec, small_in, tab, g_in):
    shape = jax.ShapeDtypeStruct
    outs = (
        shape((256, WIDTH), BF),
        shape((256, WIDTH), BF),
        shape((2, 4, 2, 24, 384), BF),
        shape((2, 2, 48, 384), BF),
        shape((16, WIDTH), F32),
    )
    dma = pltpu.SemaphoreType.DMA
    vmem = pl.BlockSpec(memory_space=pltpu.VMEM)
    return pl.pallas_call(
        back_kernel,
        name="back",
        out_shape=outs,
        in_specs=[vmem] * 14,
        out_specs=(vmem,) * len(outs),
        scratch_shapes=[
            pltpu.VMEM((4, 4, 4, 48, 384), BF),
            pltpu.VMEM((3, 512, 256), BF),
            pltpu.VMEM((3, 512, 256), BF),
            pltpu.VMEM((3, 512, 256), BF),
            pltpu.VMEM((1024, HEAD_DIM), F32),
            pltpu.VMEM((1024, HEAD_DIM), F32),
            pltpu.VMEM((2, 512, 192), BF),
            pltpu.VMEM((2, 512, 192), BF),
            pltpu.VMEM((2, 512, 384), BF),
            pltpu.VMEM((512, 384), BF),
            pltpu.VMEM((512, WIDTH), F32),
            pltpu.VMEM((2, 256, WIDTH), F32),
            pltpu.VMEM((12, 3, 4, 48, 384), BF),
            pltpu.VMEM((12, 4, 48, 384), BF),
            pltpu.VMEM((12, 3, 48, 384), BF),
            pltpu.VMEM((12, 48, 384), BF),
            pltpu.VMEM((3, 3, 48, 384), BF),
            pltpu.VMEM((2, 2, 24, 384), BF),
            pltpu.VMEM((14, 16, WIDTH), F32),
            dma((12, 3)),
            dma((12, 3)),
            dma((12, 3)),
            dma((12, 3)),
            dma((3, 3)),
            dma((3, 3)),
            dma((3,)),
            dma((3,)),
            dma((4,)),
            dma((4,)),
            dma((3, 3)),
            dma((3, 3)),
            dma((10,)),
            dma((10,)),
        ],
        compiler_params=pltpu.CompilerParams(
            collective_id=1, has_side_effects=True, vmem_limit_bytes=60 * MIB
        ),
    )(heads, ob_part, gim_part, mlp_grads, weights, p_other, xx, gh, in_attn, in_attn_t, vec, small_in, tab, g_in)


def rotary_tables(first, count):
    half = ROT_DIM // 2
    freqs = jnp.power(10000.0, -2.0 * jnp.arange(half, dtype=F32) / ROT_DIM)
    angles = (first + jnp.arange(count)).astype(F32)[:, None] * freqs[None, :]
    cosine, sine = jnp.cos(angles), jnp.sin(angles)
    ones = jnp.ones((count, HEAD_DIM - ROT_DIM), F32)
    zero_half = jnp.zeros((count, half), F32)
    cos_row = jnp.concatenate([cosine, cosine, ones], axis=1)
    left = jnp.concatenate([-sine, zero_half, ones * 0.0], axis=1)
    right = jnp.concatenate([zero_half, sine, ones * 0.0], axis=1)
    return jnp.stack([jnp.tile(t, (1, 2)) for t in (cos_row, left, right)])


def place(values, owner, count):
    each = values.shape[0]
    spots = jnp.arange(count) // each
    return jnp.where(spots == owner, jnp.tile(values, count // each), jnp.zeros((), values.dtype))


def local(
    block_in,
    cotangent,
    attn_gain,
    attn_bias,
    mlp_gain,
    mlp_bias,
    qkv_weight,
    qkv_bias,
    proj_weight,
    proj_bias,
    up_weight,
    up_bias,
    down_weight,
    down_bias,
):
    dp = lax.axis_index("dp")
    seq = lax.axis_index("seq")
    core = seq % 2

    def mine(array, axis):
        return lax.dynamic_index_in_dim(array, core, axis, keepdims=False)

    qkv = mine(qkv_weight.reshape(24, 2, 2, 3, 3, HEAD_DIM), 2)
    w_qk = qkv[:, :, :, :2, :].reshape(24, 2, 384).transpose(1, 0, 2)
    w_v = qkv[:, :, :, 2, :].reshape(1, 24, 384)
    w_p = mine(proj_weight.reshape(24, 2, 384), 1)[None]
    w_u = mine(up_weight.reshape(24, 4, 4, 2, 2, 48), 4)
    w_u = w_u.transpose(1, 0, 3, 2, 4).reshape(4, 24, 384)
    w_a = jnp.concatenate([w_qk, w_v, w_p, w_u], axis=0)
    w_d = mine(down_weight.reshape(2, 48, 2, 384), 0).transpose(1, 0, 2)

    b_qkv = mine(place(qkv_bias, dp, 2304).reshape(2, 2, 3, 3, HEAD_DIM), 1)
    b_qk = b_qkv[:, :, :2, :].reshape(768)
    b_v = b_qkv[:, :, 2, :].reshape(384)
    b_u = mine(place(up_bias, dp, 3072).reshape(4, 4, 2, 2, 48), 3)
    b_u = b_u.transpose(0, 2, 1, 3).reshape(2, 768)
    rows = [place(v, dp, 768) for v in (attn_gain, attn_bias, mlp_gain, mlp_bias, proj_bias, down_bias)]
    rows += [b_qk, jnp.concatenate([b_v, jnp.zeros((384,), BF)]), b_u[0], b_u[1]]
    rows += [jnp.zeros((768,), BF)] * 6
    vec_in = jnp.stack(rows)

    tab = rotary_tables((seq // 2) * 512, 512)
    x_in = block_in.reshape(256, WIDTH)
    g_in = cotangent.reshape(256, WIDTH)
    (heads, ob_part, gim_part, mlp_grads, weights, p_other, xx, gh, in_attn, in_attn_t, vec, small) = front(
        x_in, g_in, w_a, w_d, vec_in, tab
    )
    block_out, input_grad, owned, owned_down, small = back(
        heads, ob_part, gim_part, mlp_grads, weights, p_other, xx, gh, in_attn, in_attn_t, vec, small, tab, g_in
    )

    owned = owned.astype(F32)
    g_qk = owned[:, 0:2, 0].reshape(2, 2, 24, 3, 2, HEAD_DIM)
    g_v = owned[:, 2, 0].reshape(2, 24, 2, 3, 1, HEAD_DIM).transpose(0, 2, 1, 3, 4, 5)
    g_qkv = jnp.concatenate([g_qk, g_v], axis=4)
    g_qkv = g_qkv.transpose(2, 1, 0, 3, 4, 5).reshape(24, 2304)
    g_proj = owned[:, 3, 0].transpose(1, 0, 2).reshape(24, 768)
    g_up = owned[:, :, 1].reshape(2, 4, 24, 2, 4, 48)
    g_up = g_up.transpose(2, 1, 4, 3, 0, 5).reshape(24, 3072)
    g_down = owned_down.astype(F32).transpose(0, 2, 1, 3).reshape(96, 768)

    def part(row, each):
        return lax.dynamic_slice_in_dim(row, dp * each, each)

    bias_qk = jnp.stack([small[5], small[9]]).reshape(2, 2, 3, 2, HEAD_DIM)
    bias_v = jnp.stack([small[6, :384], small[10, :384]]).reshape(2, 2, 3, 1, HEAD_DIM)
    bias_qkv = jnp.concatenate([bias_qk, bias_v], axis=3).transpose(1, 0, 2, 3, 4).reshape(2304)
    bias_up = jnp.stack([small[7:9].reshape(1536), small[11:13].reshape(1536)])
    bias_up = bias_up.reshape(2, 4, 2, 4, 48).transpose(1, 3, 2, 0, 4).reshape(3072)
    out_total = part(small[4], 24)
    return (
        block_out.reshape(1, 256, WIDTH),
        input_grad.reshape(1, 256, WIDTH),
        part(small[0], 24),
        part(small[1], 24),
        part(small[2], 24),
        part(small[3], 24),
        g_qkv,
        part(bias_qkv, 72),
        g_proj,
        out_total,
        g_up,
        part(bias_up, 96),
        g_down,
        out_total,
    )


def solution(mesh):
    tokens = P("dp", "seq", None)
    in_specs = (tokens, tokens) + (P("dp"),) * 4 + (P("dp", None), P("dp")) * 4
    return jax.shard_map(
        local, mesh=mesh, in_specs=in_specs, out_specs=in_specs, check_vma=False
    )
```

time: 1380 us -> 192 us (0.14)
  waiting for transfers between devices: 747 us -> 0 us
  blocking collectives: 390 us -> 0 us
  Pallas kernels: 0 us -> 166 us
  matrix products: 68.2 us -> 0 us
  starting transfers between devices: 56.3 us -> 0 us
  other arithmetic: 38.6 us -> 2.5 us
  local copies, waits for them, and re-layouts: 51.2 us -> 22.3 us
  between operations: 19 us -> 1.37 us
    reduce_scatter x4 -> x0, waiting for transfers between devices: 444 us -> none  [the longest x1 170 us: local(): lax.psum_scatter(local_grads[10].astype(jnp.bfloat16), 'dp', scatter_dime...]
    unnamed x2 -> x0, blocking collectives: 267 us -> none
    all_gather x4 -> x0, waiting for transfers between devices: 247 us -> none  [the longest x1 133 us: local(): lax.all_gather(shards[10], 'dp', axis=0, tiled=True)]
    pallas_call x0 -> x2, Pallas kernels: none -> 166 us  [the longest x1 83.1 us: back(): pl.pallas_call(back_kernel, name='back', out_shape=outs, in_specs=[vmem]...]
    all_to_all x2 -> x0, blocking collectives: 82.9 us -> none  [the longest x1 46.5 us: local(): lax.all_to_all(as_sent(grad_packed.reshape(seqs_here, full_len, 1, heads_...]
    dot_general x24 -> x0, matrix products: 68.2 us -> none  [the longest x4 13.4 us: outer_sum(): jnp.einsum('rd,re->de', flat_rows(left), flat_rows(right), preferred_elem...]
    all_to_all x2 -> x0, starting transfers between devices: 55.4 us -> none  [the longest x1 30.5 us: local(): lax.all_to_all(grad_att_tokens.reshape(seqs_here, local_len, groups, head...]
    psum x1 -> x0, blocking collectives: 39.4 us -> none  [local(): lax.psum(owned[0].astype(jnp.bfloat16), 'seq').astype(jnp.float32)]
  transfers between devices with their start and end apart: 11 -> 0, of which waited for: 7 -> 0; matrix products, arithmetic and copies ran while one was open for 11% -> 0% of each run, Pallas kernels for 0% -> 0%
where the time goes in v1:
time: 192 us
  Pallas kernels  166 us (86%)
  local copies, waits for them, and re-layouts  22.3 us (12%)
  other arithmetic  2.5 us (1%)
    pallas_call x1, Pallas kernels, back(): pl.pallas_call(back_kernel, name='back', out_shape=outs, in_specs=[vmem]...  83.1 us
    pallas_call x1, Pallas kernels, front(): pl.pallas_call(front_kernel, name='front', out_shape=outs, in_specs=[vmem...  82.8 us

profile of v1, /device:TPU:1, one launch (start us, length us, event | category | flops | bytes accessed | tf_op | source)
XLA Modules:
  0.0 192.0 jit_solution(8488156214069577983)
XLA Ops:
  0.7 0.1 multiply_cosine_fusion
  0.8 0.1 pad.19.clone
  0.9 0.1 pad.22.clone
  1.0 0.1 maximum_maximum_fusion.1
  1.1 0.1 copy.63
  1.3 0.1 copy.64
  1.5 0.1 copy.65
  1.6 0.9 pad_maximum_fusion.tab
  2.6 0.4 reshape.257
  3.0 0.5 constant_dynamic-slice_fusion.7
  3.6 0.1 copy.88
  3.7 0.2 reshape.258
  3.9 0.2 reshape.254
  4.3 0.1 reshape.255
  4.4 0.1 reshape_squeeze.15
  4.6 0.7 pad_maximum_fusion.1.w_a
  5.3 0.1 tile.110
  5.5 0.1 slice.74
  5.6 0.1 slice.76
  5.7 0.1 tile.109
  5.9 0.1 reshape_squeeze.16
  6.0 0.1 stack_reshape.2
  6.1 0.1 tile.105
  6.2 0.1 tile.107
  6.4 0.1 tile.49
  6.5 0.1 tile.51
  6.6 0.1 tile.45
  6.7 0.1 tile.47
  6.9 1.3 stack.37.vec_in
  8.3 0.6 copy.90
  8.9 82.8 %front.1 = (bf16[3,2,512,256]{3,2,1,0:T(8,128)(2,1)}, f32[512,768]{1,0:T(8,128)}, f32[512,768]{1,0:T(8,128)}, bf16[8,4,4,48,384]{4,3,2,1,0:T(8,128)(2,1)}, bf16[...) custom-call(bf16[256,768]{1,0:T(8,128)(2,1)} %bitcast.83, ...), custom_call_target="tpu_custom_call" | custom-call | tf_op jit(solution)/shard_map/front/pallas_call | solution.py:398
  91.7 83.1 %back.1 = (bf16[256,768]{1,0:T(8,128)(2,1)}, bf16[256,768]{1,0:T(8,128)(2,1)}, bf16[2,4,2,24,384]{4,3,2,1,0:T(8,128)(2,1)}, bf16[2,2,48,384]{3,2,1,0:T(8,128)(2,1)}, f32[16,768]{1,0:T(8,128)}) custom-call(bf16[3,2,512,256]{3,2,1,0:T(8,128)(2,1)} %get-tuple-element.31.heads, f32[512,768]{1,0:T(8,128)} %get-tuple-element.32.ob_part, ...), custom_call_target="tpu_custom_call" | custom-call | tf_op jit(solution)/shard_map/back/pallas_call | solution.py:862
  174.8 0.8 fusion.14
  175.6 0.1 stack.41
  175.7 0.1 stack.42
  175.9 0.1 reshape.268
  176.0 0.6 dynamic_slice.72
  176.6 1.0 fusion.15
  177.5 0.1 reshape.263
  177.6 0.7 fusion.16
  178.4 0.1 reshape.264
  178.5 0.1 reshape.265
  178.6 0.6 dynamic_slice.69
  179.2 0.9 slice.98
  180.1 0.2 reshape_squeeze.17
  180.3 0.8 slice.99
  181.1 0.1 reshape_squeeze.18
  181.2 0.2 copy.67
  181.4 0.3 maximum_bitcast_fusion
  181.7 1.1 reshape.262
  182.8 0.7 reshape_squeeze.19
  183.5 0.6 copy.71
  184.1 1.8 reshape.267
  186.0 0.2 copy.74
  186.1 0.7 copy.78
  186.9 0.6 copy.77
  187.5 0.1 fusion.13
  187.6 0.6 fusion.10
  188.2 0.6 fusion.11
  188.8 0.6 fusion.12
  189.4 0.6 fusion.9
  189.9 0.5 copy.96
  190.5 0.7 copy.97
  191.2 0.7 copy.98
  (89 shorter events, 1.0 us)
Async XLA Ops:
  1.3 1.3 copy-start.5
  1.6 2.3 %copy-start.6 = (bf16[24,2304]{1,0:T(8,128)(2,1)S(1)}, bf16[24,2304]{1,0:T(8,128)(2,1)}, u32[]{:S(2)}) copy-start(bf16[24,2304]{1,0:T(8,128)(2,1)} %param.20) | copy-start | bytes 331780
  3.0 1.6 copy-start.7
  3.5 1.8 copy-start.15
  3.5 2.2 %copy-start.8 = (bf16[72]{0:T(256)(128)(2,1)S(1)}, bf16[72]{0:T(256)(128)(2,1)}, u32[]{:S(2)}) copy-start(bf16[72]{0:T(256)(128)(2,1)} %param.21) | copy-start | bytes 436
  3.5 2.6 %copy-start.9 = (bf16[24]{0:T(256)(128)(2,1)S(1)}, bf16[24]{0:T(256)(128)(2,1)}, u32[]{:S(2)}) copy-start(bf16[24]{0:T(256)(128)(2,1)} %param.23) | copy-start | bytes 148
  3.5 2.7 %copy-start.10 = (bf16[24]{0:T(256)(128)(2,1)S(1)}, bf16[24]{0:T(256)(128)(2,1)}, u32[]{:S(2)}) copy-start(bf16[24]{0:T(256)(128)(2,1)} %param.27) | copy-start | bytes 148
  3.5 2.8 %copy-start.11 = (bf16[24]{0:T(256)(128)(2,1)S(1)}, bf16[24]{0:T(256)(128)(2,1)}, u32[]{:S(2)}) copy-start(bf16[24]{0:T(256)(128)(2,1)} %param.18) | copy-start | bytes 148
  3.5 2.9 %copy-start.12 = (bf16[24]{0:T(256)(128)(2,1)S(1)}, bf16[24]{0:T(256)(128)(2,1)}, u32[]{:S(2)}) copy-start(bf16[24]{0:T(256)(128)(2,1)} %param.19) | copy-start | bytes 148
  3.5 3.1 %copy-start.13 = (bf16[24]{0:T(256)(128)(2,1)S(1)}, bf16[24]{0:T(256)(128)(2,1)}, u32[]{:S(2)}) copy-start(bf16[24]{0:T(256)(128)(2,1)} %param.16) | copy-start | bytes 148
  3.6 3.2 %copy-start.14 = (bf16[24]{0:T(256)(128)(2,1)S(1)}, bf16[24]{0:T(256)(128)(2,1)}, u32[]{:S(2)}) copy-start(bf16[24]{0:T(256)(128)(2,1)} %param.17) | copy-start | bytes 148
  3.6 4.6 %copy-start.4 = (bf16[96,768]{1,0:T(8,128)(2,1)S(1)}, bf16[96,768]{1,0:T(8,128)(2,1)}, u32[]{:S(2)}) copy-start(bf16[96,768]{1,0:T(8,128)(2,1)} %param.26) | copy-start | bytes 442372
  180.1 2.7 %copy-start = (bf16[2,4,2,24,384]{4,3,2,1,0:T(8,128)(2,1)S(1)}, bf16[2,4,2,24,384]{4,3,2,1,0:T(8,128)(2,1)}, u32[]{:S(2)}) copy-start(bf16[2,4,2,24,384]{4,3,2,1,0:T(8,128)(2,1)} %get-tuple-element.46) | copy-start | bytes 884740
  183.4 2.5 %copy-start.3 = (bf16[2,2,48,384]{3,2,1,0:T(8,128)(2,1)S(1)}, bf16[2,2,48,384]{3,2,1,0:T(8,128)(2,1)}, u32[]{:S(2)}) copy-start(bf16[2,2,48,384]{3,2,1,0:T(8,128)(2,1)} %get-tuple-element.47) | copy-start | bytes 442372
  185.9 4.5 %copy-start.2 = (bf16[256,768]{1,0:T(8,128)(2,1)S(1)}, bf16[256,768]{1,0:T(8,128)(2,1)}, u32[]{:S(2)}) copy-start(bf16[256,768]{1,0:T(8,128)(2,1)} %get-tuple-element.43) | copy-start | bytes 1179652
  185.9 5.3 %copy-start.1 = (bf16[256,768]{1,0:T(8,128)(2,1)S(1)}, bf16[256,768]{1,0:T(8,128)(2,1)}, u32[]{:S(2)}) copy-start(bf16[256,768]{1,0:T(8,128)(2,1)} %get-tuple-element.44) | copy-start | bytes 1179652
  187.6 4.3 %copy-start.16 = (f32[24]{0:T(128)}, f32[24]{0:T(128)S(1)}, u32[]{:S(2)}) copy-start(f32[24]{0:T(128)S(1)} %fusion.13) | copy-start | bytes 292

commit v2 on v0

v2 whole, which is shorter than its diff:
```python
import math

import jax
import jax.numpy as jnp
import numpy as np
from jax import lax
from jax.experimental import pallas as pl
from jax.experimental.pallas import tpu as pltpu
from jax.sharding import PartitionSpec as P

HEADS = 12
HEAD_DIM = 64
ROT_DIM = 16
WIDTH = 768
EPSILON = 1e-05
MASKED = -1e30
MESH = pl.DeviceIdType.MESH
BF = jnp.bfloat16
F32 = jnp.float32
MIB = 1 << 20


def coords():
    dp = lax.axis_index("dp")
    seq = lax.axis_index("seq")
    x = lax.div(dp, 8)
    y = lax.rem(lax.div(dp, 2), 4)
    z_lo = lax.rem(dp, 2)
    z_hi = lax.div(seq, 2)
    core = lax.rem(seq, 2)
    return x, y, z_hi * 2 + z_lo, core


def device(x, y, z, core):
    return (x * 8 + y * 2 + lax.rem(z, 2), lax.div(z, 2) * 2 + core)


def around(at, offset):
    return lax.rem(at + offset, 4)


def copy_to(src, dst, send_sem, recv_sem, target):
    return pltpu.make_async_remote_copy(
        src_ref=src,
        dst_ref=dst,
        send_sem=send_sem,
        recv_sem=recv_sem,
        device_id=target,
        device_id_type=MESH,
    )


def dot(left, right):
    return jnp.dot(left, right, preferred_element_type=F32)


def dot_t(left, right):
    return lax.dot_general(left, right, (((1,), (1,)), ((), ())), preferred_element_type=F32)


def dot_a(left, right):
    return lax.dot_general(left, right, (((0,), (0,)), ((), ())), preferred_element_type=F32)


def greet(targets):
    barrier = pltpu.get_barrier_semaphore()
    for target in targets:
        pl.semaphore_signal(barrier, inc=1, device_id=target, device_id_type=MESH)
    pl.semaphore_wait(barrier, len(targets))


def weight_rows(ref):
    value = ref[...]
    return value.reshape(value.shape[0] * value.shape[1] * value.shape[2], value.shape[3])


def slab_rows(value):
    return value.reshape(value.shape[0] * value.shape[1], value.shape[2])


N_BLOCK = 6
QK, VP = 4, 5


def whole_kernel(
    x_in,
    g_in,
    w_a,
    vec_in,
    tab,
    block_out,
    input_grad,
    owned,
    small,
    weights,
    vecs,
    z_a,
    z_v,
    vec,
    xx,
    gg,
    normed,
    in_attn,
    in_attn_t,
    in_mlp,
    in_mlp_t,
    activ,
    low_grad,
    ob_part,
    gim_part,
    grads,
    p_send,
    p_recv,
    p_rows,
    qk_rows,
    vd_rows,
    dk_acc,
    dv_acc,
    att,
    grad_qk,
    grad_v,
    pg_send,
    pg_recv,
    r_one,
    mid,
    r_two,
    kept,
    z_send,
    z_recv,
    sums,
    swap_f,
    swap_r,
    far_b,
    far_r,
    small_b,
    small_r,
    pair_ss,
    pair_rs,
    tok_ss,
    tok_rs,
    one_ss,
    one_rs,
    two_ss,
    two_rs,
    p_ss,
    p_rs,
    sone_ss,
    sone_rs,
    stwo_ss,
    stwo_rs,
    z_ss,
    z_rs,
    share_ss,
    share_rs,
    swap_ss,
    swap_rs,
    small_ss,
    small_rs,
):
    x, y, z, core = coords()
    z_lo = lax.rem(z, 2)
    z_hi = lax.div(z, 2)
    me = z_hi * 2 + core
    x_peers = [device(around(x, o), y, z, core) for o in (1, 2, 3)]
    y_peers = [device(x, around(y, o), z, core) for o in (1, 2, 3)]
    z_far = around(z, 2)
    sibling = device(x, y, z, 1 - core)
    far = device(x, y, z_far, core)
    cross = device(x, y, z_far, 1 - core)
    z_pair = device(x, y, z_hi * 2 + 1 - z_lo, core)
    group = [sibling, far, cross]
    group_ids = [z_hi * 2 + 1 - core, (1 - z_hi) * 2 + core, (1 - z_hi) * 2 + 1 - core]
    greet(x_peers + y_peers + group + [z_pair])

    def token_rows(index):
        return pl.ds(pl.multiple_of(index * 256, 256), 256)

    def start(copies):
        for item in copies:
            item.start()

    pair = [copy_to(vec_in, z_v, pair_ss.at[0], pair_rs.at[0], z_pair)]
    for k in range(3):
        part = pl.ds(2 * k, 2)
        pair.append(
            copy_to(w_a.at[part], z_a.at[part], pair_ss.at[1 + k], pair_rs.at[1 + k], z_pair)
        )
    start([pair[1], pair[0], pair[2], pair[3]])

    mine = token_rows(me)
    theirs = token_rows(group_ids[1])
    tokens = []
    for k, (source, held) in enumerate(((x_in, xx), (g_in, gg))):
        tokens.append(
            (
                copy_to(source, held.at[mine], tok_ss.at[k, 0], tok_rs.at[k, 0], sibling),
                copy_to(source, held.at[mine], tok_ss.at[k, 1], tok_rs.at[k, 1], far),
                copy_to(held.at[theirs], held.at[theirs], tok_ss.at[k, 2], tok_rs.at[k, 2], sibling),
            )
        )
    for k in range(2):
        tokens[k][1].start()
        tokens[k][0].start()
    xx[mine, :] = x_in[...]
    gg[mine, :] = g_in[...]

    def assemble(i):
        own = w_a[i].astype(F32)
        other = z_a[i].astype(F32)
        first = z_lo == 0
        weights[i, x, y] = jnp.concatenate(
            [jnp.where(first, own, other), jnp.where(first, other, own)], axis=0
        ).astype(BF)

    def gather_ref(i):
        return vecs if i == N_BLOCK else weights.at[i]

    def gather(i, number, arriving=False):
        ref = gather_ref(i)
        along_y = (i % 2 == 0) == (number == 1)
        ss, rs = (one_ss, one_rs) if number == 1 else (two_ss, two_rs)
        copies = []
        for k, o in enumerate((1, 2, 3)):
            target = y_peers[k] if along_y else x_peers[k]
            xs, ys = x, y
            if arriving and along_y:
                ys = around(y, 4 - o)
            elif arriving:
                xs = around(x, 4 - o)
            if number == 1:
                part = ref.at[xs, ys]
            elif along_y:
                part = ref.at[:, ys]
            else:
                part = ref.at[xs]
            copies.append(copy_to(part, part, ss.at[i, k], rs.at[i, k], target))
        return copies

    def arrived(i, number):
        for item in gather(i, number, True):
            item.wait_recv()

    def layer_norm(index):
        for step in range(2):
            rows = pl.ds(pl.multiple_of(index * 256 + step * 128, 128), 128)
            values = xx[rows, :].astype(F32)
            center = values - jnp.mean(values, axis=-1, keepdims=True)
            inv_std = lax.rsqrt(jnp.mean(center * center, axis=-1, keepdims=True) + EPSILON)
            normed[rows, :] = center * inv_std

    pair[1].wait_recv()
    assemble(0)
    assemble(1)
    start(gather(0, 1) + gather(1, 1))
    pair[0].wait_recv()
    vecs[x, y] = (vec_in[...].astype(F32) + z_v[...].astype(F32)).astype(BF)
    start(gather(N_BLOCK, 1))
    pair[2].wait_recv()
    assemble(2)
    assemble(3)
    start(gather(2, 1) + gather(3, 1))
    pair[3].wait_recv()
    assemble(4)
    assemble(5)
    start(gather(4, 1) + gather(5, 1))
    layer_norm(me)
    for i in (0, 1, N_BLOCK, 2, 3, 4, 5):
        arrived(i, 1)
        start(gather(i, 2))
    tokens[0][0].wait_recv()
    layer_norm(group_ids[0])
    tokens[0][1].wait_recv()
    tokens[0][2].start()
    layer_norm(group_ids[1])
    tokens[0][2].wait_recv()
    layer_norm(group_ids[2])
    arrived(N_BLOCK, 2)
    total = jnp.zeros((16, WIDTH), F32)
    for i in range(4):
        for j in range(4):
            total = total + vecs[i, j].astype(F32)
    vec[...] = total

    @pl.loop(0, 4)
    def _(step):
        rows = token_rows(step)
        values = normed[rows, :]
        attn_rows = (values * vec[0:1, :] + vec[1:2, :]).astype(BF)
        mlp_rows = (values * vec[2:3, :] + vec[3:4, :]).astype(BF)
        in_attn[rows, :] = attn_rows
        in_mlp[rows, :] = mlp_rows
        in_attn_t[:, rows] = attn_rows.T
        in_mlp_t[:, rows] = mlp_rows.T

    tokens[1][1].wait_recv()
    tokens[1][2].start()
    tokens[1][0].wait_recv()
    arrived(0, 2)
    arrived(1, 2)
    arrived(2, 2)
    arrived(3, 2)
    tokens[1][2].wait_recv()

    def first_copies(i):
        ref = grads.at[i]
        copies = []
        for k, o in enumerate((1, 2, 3)):
            if i % 2 == 0:
                part, target = ref.at[around(x, o)], x_peers[k]
            else:
                part, target = ref.at[:, around(y, o)], y_peers[k]
            copies.append(
                copy_to(part, r_one.at[i, k], sone_ss.at[i, k], sone_rs.at[i, k], target)
            )
        return copies

    def second_copies(i):
        copies = []
        for k, o in enumerate((1, 2, 3)):
            if i % 2 == 0:
                part, target = mid.at[i, around(y, o)], y_peers[k]
            else:
                part, target = mid.at[i, around(x, o)], x_peers[k]
            copies.append(
                copy_to(part, r_two.at[i, k], stwo_ss.at[i, k], stwo_rs.at[i, k], target)
            )
        return copies

    def pair_copy(i):
        return copy_to(z_send.at[i], z_recv.at[i], z_ss.at[i], z_rs.at[i], z_pair)

    def share_copies(number):
        part = owned.at[me, pl.ds(0, 4)] if number == 0 else owned.at[me, pl.ds(4, 2)]
        return [
            copy_to(part, part, share_ss.at[number, k], share_rs.at[number, k], group[k])
            for k in range(3)
        ]

    def share_arrived(number):
        for k in range(3):
            at = group_ids[k]
            part = owned.at[at, pl.ds(0, 4)] if number == 0 else owned.at[at, pl.ds(4, 2)]
            copy_to(
                part, part, share_ss.at[number, k], share_rs.at[number, k], group[k]
            ).wait_recv()

    def first_sum(i):
        for item in first_copies(i):
            item.wait_recv()

        @pl.loop(0, 4)
        def _(j):
            own = grads[i, x, j] if i % 2 == 0 else grads[i, j, y]
            total = own.astype(F32)
            for k in range(3):
                total = total + r_one[i, k, j].astype(F32)
            mid[i, j] = total.astype(BF)

        start(second_copies(i))

    def second_sum(i):
        for item in second_copies(i):
            item.wait_recv()
        total = mid[i, y if i % 2 == 0 else x].astype(F32)
        for k in range(3):
            total = total + r_two[i, k].astype(F32)
        first = z_lo == 0
        kept[i] = jnp.where(first, total[:24], total[24:])
        z_send[i] = jnp.where(first, total[24:], total[:24]).astype(BF)
        pair_copy(i).start()

    def third_sum(i):
        pair_copy(i).wait_recv()
        owned[me, i] = (kept[i] + z_recv[i].astype(F32)).astype(BF)

    def p_copies(sent, received, number):
        return [
            copy_to(
                sent.at[group_ids[k]],
                received.at[me],
                p_ss.at[number, k],
                p_rs.at[number, k],
                group[k],
            )
            for k in range(3)
        ]

    def p_arrived(sent, received, number):
        for k in range(3):
            copy_to(
                sent.at[0],
                received.at[group_ids[k]],
                p_ss.at[number, k],
                p_rs.at[number, k],
                group[k],
            ).wait_recv()

    for b in range(2):
        weight_up = weight_rows(weights.at[b])
        down = [
            weights[2 + half, 2 * b : 2 * b + 2].reshape(384, 384) for half in range(2)
        ]

        @pl.loop(0, 4)
        def _(step):
            rows = token_rows(step)
            up_pre = dot(in_mlp[rows, :], weight_up) + vec[7:8, b * 384 : b * 384 + 384]
            cdf = 0.5 * (1.0 + lax.erf(up_pre * (1.0 / math.sqrt(2.0))))
            act = (up_pre * cdf).astype(BF)
            density = jnp.exp(-0.5 * up_pre * up_pre) * (1.0 / math.sqrt(2.0 * math.pi))
            slope = cdf + up_pre * density
            grad_activ = dot_t(gg[rows, :384], down[0]) + dot_t(gg[rows, 384:], down[1])
            grad_up = (grad_activ * slope).astype(BF)
            activ[rows, :] = act
            low_grad[rows, :] = grad_up
            for half in range(2):
                cols = slice(half * 384, half * 384 + 384)
                out = dot(act, down[half])
                if b:
                    out = out + ob_part[rows, cols]
                ob_part[rows, cols] = out
            back = dot_t(grad_up, weight_up)
            if b:
                back = back + gim_part[rows, :]
            gim_part[rows, :] = back

        grads[b] = dot(in_mlp_t[...], low_grad[...]).astype(BF).reshape(4, 4, 48, 384)
        start(first_copies(b))
        small_b[6:7, b * 384 : b * 384 + 384] = jnp.sum(
            low_grad[...].astype(F32), axis=0, keepdims=True
        )
        activ_t = activ[...].T
        for half in range(2):
            grad_down = dot(activ_t, gg[:, half * 384 : half * 384 + 384]).astype(BF)
            grads[2 + half, 2 * b : 2 * b + 2] = grad_down.reshape(2, 4, 48, 384)
        if b == 0:
            arrived(VP, 2)
            for k in range(4):
                p_send[k] = weights[VP, k].reshape(192, 384)[:, 192:]
            start(p_copies(p_send, p_recv, 0))
            p_recv[me] = p_send[me]
    start(first_copies(2) + first_copies(3))

    grad_in = gim_part[...]
    small_b[2:3, :] = jnp.sum(grad_in * normed[...], axis=0, keepdims=True)
    small_b[3:4, :] = jnp.sum(grad_in, axis=0, keepdims=True)
    small_b[4:5, :] = jnp.sum(g_in[...].astype(F32), axis=0, keepdims=True)
    small_b[7:8, :] = jnp.zeros((1, WIDTH), F32)

    p_arrived(p_send, p_recv, 0)
    for k in range(4):
        p_rows[:, k * 192 : k * 192 + 192] = p_recv[k]
    arrived(QK, 2)

    @pl.loop(0, 4)
    def _(step):
        rows = token_rows(step)
        activations = in_attn[rows, :]
        pre = dot(activations, weight_rows(weights.at[QK])) + vec[6:7, :384]
        value_pre = dot(activations, weight_rows(weights.at[VP])[:, :192]) + vec[6:7, 384:576]
        value_pre = value_pre.astype(BF)
        grad_att = dot_t(gg[rows, :], p_rows[...]).astype(BF)
        for head in range(3):
            part = pre[:, head * 128 : head * 128 + 128]
            qk_rows[head, rows, :] = (
                part * tab[0, rows, :]
                + pltpu.roll(part, 120, 1) * tab[1, rows, :]
                + pltpu.roll(part, 8, 1) * tab[2, rows, :]
            ).astype(BF)
            at = slice(head * 64, head * 64 + 64)
            vd_rows[head, rows, :] = jnp.concatenate([value_pre[:, at], grad_att[:, at]], axis=1)

    scale = 1.0 / math.sqrt(HEAD_DIM)

    def attend(head):
        queries = qk_rows[head, :, 0:64]
        key_rows = qk_rows[head, :, 64:128]
        value_rows = vd_rows[head, :, 0:64]
        grad_rows = vd_rows[head, :, 64:128]
        dk_acc[...] = jnp.zeros((1024, HEAD_DIM), F32)
        dv_acc[...] = jnp.zeros((1024, HEAD_DIM), F32)
        dq_parts = []
        for blk in range(4):
            lo, hi = blk * 256, blk * 256 + 256
            q = queries[lo:hi]
            do = grad_rows[lo:hi]
            scores = dot_t(q, key_rows[:hi]) * scale
            row_place = lax.broadcasted_iota(jnp.int32, (256, hi), 0) + lo
            col_place = lax.broadcasted_iota(jnp.int32, (256, hi), 1)
            scores = jnp.where(row_place >= col_place, scores, MASKED)
            peak = jnp.max(scores, axis=-1, keepdims=True)
            expo = jnp.exp(scores - peak)
            probs = expo * (1.0 / jnp.sum(expo, axis=-1, keepdims=True))
            low_probs = probs.astype(BF)
            att[lo:hi, head * 64 : head * 64 + 64] = dot(low_probs, value_rows[:hi]).astype(BF)
            grad_probs = dot_t(do, value_rows[:hi])
            inner = jnp.sum(probs * grad_probs, axis=-1, keepdims=True)
            grad_scores = (probs * (grad_probs - inner)).astype(BF)
            dq_parts.append((dot(grad_scores, key_rows[:hi]) * scale).astype(BF))
            dk_acc[:hi, :] += dot_a(grad_scores, q)
            dv_acc[:hi, :] += dot_a(low_probs, do)
        dk = (dk_acc[...] * scale).astype(BF)
        dq = jnp.concatenate(dq_parts, axis=0)
        grad_v[:, head * 64 : head * 64 + 64] = dv_acc[...].astype(BF)
        part = jnp.concatenate([dq, dk], axis=1).astype(F32)
        grad_qk[:, head * 128 : head * 128 + 128] = (
            part * tab[0]
            - pltpu.roll(part, 120, 1) * tab[1]
            - pltpu.roll(part, 8, 1) * tab[2]
        ).astype(BF)

    attend(0)
    first_sum(0)
    first_sum(1)
    attend(1)
    first_sum(2)
    first_sum(3)
    second_sum(0)
    second_sum(1)
    attend(2)
    second_sum(2)
    second_sum(3)

    def grad_chunk(index, number):
        rows = token_rows(index)
        grad_in = dot_t(grad_qk[rows, :], weight_rows(weights.at[QK])) + dot_t(
            grad_v[rows, :], weight_rows(weights.at[VP])[:, :192]
        )
        bias = jnp.sum(grad_in, axis=0, keepdims=True)
        gain = jnp.sum(grad_in * normed[rows, :], axis=0, keepdims=True)
        if number:
            bias = bias + small_b[1:2, :]
            gain = gain + small_b[0:1, :]
        small_b[1:2, :] = bias
        small_b[0:1, :] = gain
        return grad_in * vec[0:1, :] + gim_part[rows, :] * vec[2:3, :]

    def out_chunk(index):
        rows = token_rows(index)
        return ob_part[rows, :] + dot(att[rows, :], p_rows[...])

    def swap(k):
        return copy_to(swap_f.at[k], swap_r.at[k], swap_ss.at[k], swap_rs.at[k], sibling)

    def far_swap(k):
        return copy_to(far_b.at[k], far_r.at[k], swap_ss.at[4 + k], swap_rs.at[4 + k], far)

    swap_f[0] = grad_chunk(group_ids[2], 0)
    swap(0).start()
    grads[QK] = dot(in_attn_t[...], grad_qk[...]).astype(BF).reshape(4, 4, 48, 384)
    start(first_copies(QK))
    grad_p = dot_a(att[...], gg[...]).astype(BF)
    for k in range(4):
        pg_send[k] = grad_p[:, k * 192 : k * 192 + 192]
    start(p_copies(pg_send, pg_recv, 1))
    pg_recv[me] = pg_send[me]
    near_sum = grad_chunk(group_ids[1], 1)
    swap(0).wait_recv()
    far_b[0] = (near_sum + swap_r[0]).astype(BF)
    far_swap(0).start()
    swap_f[1] = out_chunk(group_ids[2])
    swap(1).start()
    for i in range(4):
        third_sum(i)
    start(share_copies(0))
    grad_value_w = dot(in_attn_t[...], grad_v[...]).astype(BF)
    p_arrived(pg_send, pg_recv, 1)
    for k in range(4):
        grads[VP, k] = jnp.concatenate(
            [grad_value_w[k * 192 : k * 192 + 192], pg_recv[k]], axis=1
        ).reshape(4, 48, 384)
    start(first_copies(VP))
    out_sum = out_chunk(group_ids[1])
    swap(1).wait_recv()
    far_b[1] = (out_sum + swap_r[1]).astype(BF)
    far_swap(1).start()
    swap_f[2] = grad_chunk(group_ids[0], 2)
    swap(2).start()
    swap_f[3] = out_chunk(group_ids[0])
    swap(3).start()
    sums[0] = grad_chunk(me, 3)
    sums[1] = out_chunk(me)
    small_b[5:6, 0:384] = jnp.sum(grad_qk[...].astype(F32), axis=0, keepdims=True)
    small_b[5:6, 384:576] = jnp.sum(grad_v[...].astype(F32), axis=0, keepdims=True)
    small_b[5:6, 576:768] = jnp.zeros((1, 192), F32)

    def small_copies(number):
        peers = (x_peers, y_peers, [z_pair])[number]
        return [
            copy_to(
                small_r.at[7 + number],
                small_r.at[number * 3 + k],
                small_ss.at[number, k],
                small_rs.at[number, k],
                peers[k],
            )
            for k in range(len(peers))
        ]

    def small_sum(number):
        total = small_r[7 + number]
        for k, item in enumerate(small_copies(number)):
            item.wait_recv()
            total = total + small_r[number * 3 + k]
        return total

    def small_share(k):
        return copy_to(
            small.at[me], small.at[me], small_ss.at[3, k], small_rs.at[3, k], group[k]
        )

    small_r[7] = small_b[...]
    start(small_copies(0))
    first_sum(QK)
    small_r[8] = small_sum(0)
    start(small_copies(1))
    first_sum(VP)
    second_sum(QK)
    small_r[9] = small_sum(1)
    start(small_copies(2))
    second_sum(VP)
    small[me] = small_sum(2)
    for k in range(3):
        small_share(k).start()
    third_sum(QK)
    third_sum(VP)
    start(share_copies(1))

    swap(2).wait_recv()
    far_swap(0).wait_recv()
    values = x_in[...].astype(F32)
    center = values - jnp.mean(values, axis=-1, keepdims=True)
    inv_std = lax.rsqrt(jnp.mean(center * center, axis=-1, keepdims=True) + EPSILON)
    norm_rows = center * inv_std
    grad_norm = sums[0] + swap_r[2] + far_r[0].astype(F32)
    input_grad[...] = (
        g_in[...].astype(F32)
        + inv_std
        * (
            grad_norm
            - jnp.mean(grad_norm, axis=-1, keepdims=True)
            - norm_rows * jnp.mean(grad_norm * norm_rows, axis=-1, keepdims=True)
        )
    ).astype(BF)
    swap(3).wait_recv()
    far_swap(1).wait_recv()
    block_out[...] = (
        values + sums[1] + swap_r[3] + far_r[1].astype(F32) + (vec[4:5, :] + vec[5:6, :])
    ).astype(BF)

    share_arrived(0)
    share_arrived(1)
    for k in range(3):
        copy_to(
            small.at[group_ids[k]],
            small.at[group_ids[k]],
            small_ss.at[3, k],
            small_rs.at[3, k],
            group[k],
        ).wait_recv()
    sent = pair + [item for three in tokens for item in three]
    for i in range(N_BLOCK + 1):
        sent += gather(i, 1) + gather(i, 2)
    for i in range(N_BLOCK):
        sent += first_copies(i) + second_copies(i) + [pair_copy(i)]
    sent += p_copies(p_send, p_recv, 0) + p_copies(pg_send, pg_recv, 1)
    sent += share_copies(0) + share_copies(1) + [small_share(k) for k in range(3)]
    sent += [swap(k) for k in range(4)] + [far_swap(k) for k in range(2)]
    for number in range(3):
        sent += small_copies(number)
    for item in sent:
        item.wait_send()


def whole(x_in, g_in, w_a, vec_in, tab):
    shape = jax.ShapeDtypeStruct
    outs = (
        shape((256, WIDTH), BF),
        shape((256, WIDTH), BF),
        shape((4, N_BLOCK, 24, 384), BF),
        shape((4, 8, WIDTH), F32),
    )
    dma = pltpu.SemaphoreType.DMA
    vmem = pl.BlockSpec(memory_space=pltpu.VMEM)
    rows = 1024
    buffers = [
        ((N_BLOCK, 4, 4, 48, 384), BF),
        ((4, 4, 16, WIDTH), BF),
        ((N_BLOCK, 24, 384), BF),
        ((16, WIDTH), BF),
        ((16, WIDTH), F32),
        ((rows, WIDTH), BF),
        ((rows, WIDTH), BF),
        ((rows, WIDTH), F32),
        ((rows, WIDTH), BF),
        ((WIDTH, rows), BF),
        ((rows, WIDTH), BF),
        ((WIDTH, rows), BF),
        ((rows, 384), BF),
        ((rows, 384), BF),
        ((rows, WIDTH), F32),
        ((rows, WIDTH), F32),
        ((N_BLOCK, 4, 4, 48, 384), BF),
        ((4, 192, 192), BF),
        ((4, 192, 192), BF),
        ((192, WIDTH), BF),
        ((3, rows, 128), BF),
        ((3, rows, 128), BF),
        ((rows, HEAD_DIM), F32),
        ((rows, HEAD_DIM), F32),
        ((rows, 192), BF),
        ((rows, 384), BF),
        ((rows, 192), BF),
        ((4, 192, 192), BF),
        ((4, 192, 192), BF),
        ((N_BLOCK, 3, 4, 48, 384), BF),
        ((N_BLOCK, 4, 48, 384), BF),
        ((N_BLOCK, 3, 48, 384), BF),
        ((N_BLOCK, 24, 384), F32),
        ((N_BLOCK, 24, 384), BF),
        ((N_BLOCK, 24, 384), BF),
        ((2, 256, WIDTH), F32),
        ((4, 256, WIDTH), F32),
        ((4, 256, WIDTH), F32),
        ((2, 256, WIDTH), BF),
        ((2, 256, WIDTH), BF),
        ((8, WIDTH), F32),
        ((10, 8, WIDTH), F32),
    ]
    sems = [
        (4,),
        (2, 3),
        (N_BLOCK + 1, 3),
        (N_BLOCK + 1, 3),
        (2, 3),
        (N_BLOCK, 3),
        (N_BLOCK, 3),
        (N_BLOCK,),
        (2, 3),
        (6,),
        (4, 3),
    ]
    scratch = [pltpu.VMEM(*item) for item in buffers]
    for item in sems:
        scratch += [dma(item), dma(item)]
    return pl.pallas_call(
        whole_kernel,
        name="whole",
        out_shape=outs,
        in_specs=[vmem] * 5,
        out_specs=(vmem,) * len(outs),
        scratch_shapes=scratch,
        compiler_params=pltpu.CompilerParams(
            collective_id=0, has_side_effects=True, vmem_limit_bytes=60 * MIB
        ),
    )(x_in, g_in, w_a, vec_in, tab)


def finish_kernel(
    out_in,
    grad_in,
    owned,
    small,
    block_out,
    input_grad,
    attn_gain_g,
    attn_bias_g,
    mlp_gain_g,
    mlp_bias_g,
    qkv_g,
    qkv_bias_g,
    proj_g,
    proj_bias_g,
    up_g,
    up_bias_g,
    down_g,
    down_bias_g,
):
    block_out[...] = out_in[...]
    input_grad[...] = grad_in[...]
    up_parts = []
    for g in range(4):
        qk = owned[g, QK].astype(F32)
        vp = owned[g, VP].astype(F32)
        for head in range(3):
            at = 576 * g + 192 * head
            qkv_g[:, at : at + 128] = qk[:, head * 128 : head * 128 + 128]
            qkv_g[:, at + 128 : at + 192] = vp[:, head * 64 : head * 64 + 64]
        proj_g[:, 192 * g : 192 * g + 192] = vp[:, 192:]
        for half in range(2):
            down_g[24 * g : 24 * g + 24, half * 384 : half * 384 + 384] = owned[
                g, 2 + half
            ].astype(F32)
        up_parts.append([owned[g, 0].astype(F32), owned[g, 1].astype(F32)])
    for d in range(32):
        at = (d % 16) * 24
        up_g[:, 96 * d : 96 * d + 96] = jnp.concatenate(
            [up_parts[g][d // 16][:, at : at + 24] for g in range(4)], axis=1
        )

    dp = lax.axis_index("dp")
    totals = small[0] + small[1] + small[2] + small[3]
    rows = jnp.concatenate(
        [totals] + [small[g, 6:7, :] for g in range(4)] + [jnp.zeros((4, WIDTH), F32)], axis=0
    )

    def pick(values, each):
        size = values.shape[1]
        row = lax.broadcasted_iota(jnp.int32, (size, each), 0)
        col = lax.broadcasted_iota(jnp.int32, (size, each), 1)
        chosen = (row == col + dp * each).astype(F32)
        return jnp.dot(
            values, chosen, precision=lax.Precision.HIGHEST, preferred_element_type=F32
        )

    picked = pick(rows, 24)
    attn_gain_g[...] = picked[0:1]
    attn_bias_g[...] = picked[1:2]
    mlp_gain_g[...] = picked[2:3]
    mlp_bias_g[...] = picked[3:4]
    proj_bias_g[...] = picked[4:5]
    down_bias_g[...] = picked[4:5]
    up_bias_g[...] = jnp.concatenate([picked[8 + g : 9 + g] for g in range(4)], axis=1)
    pieces = []
    for g in range(4):
        for head in range(3):
            pieces.append(small[g, 5:6, head * 128 : head * 128 + 128])
            pieces.append(small[g, 5:6, 384 + head * 64 : 384 + head * 64 + 64])
    bias = jnp.concatenate(pieces, axis=1)
    qkv_bias_g[...] = pick(jnp.broadcast_to(bias, (8, 2304)), 72)[0:1]


def finish(out_in, grad_in, owned, small):
    shape = jax.ShapeDtypeStruct
    outs = (
        shape((256, WIDTH), BF),
        shape((256, WIDTH), BF),
        shape((1, 24), F32),
        shape((1, 24), F32),
        shape((1, 24), F32),
        shape((1, 24), F32),
        shape((24, 2304), F32),
        shape((1, 72), F32),
        shape((24, 768), F32),
        shape((1, 24), F32),
        shape((24, 3072), F32),
        shape((1, 96), F32),
        shape((96, 768), F32),
        shape((1, 24), F32),
    )
    vmem = pl.BlockSpec(memory_space=pltpu.VMEM)
    return pl.pallas_call(
        finish_kernel,
        name="finish",
        out_shape=outs,
        in_specs=[vmem] * 4,
        out_specs=(vmem,) * len(outs),
        compiler_params=pltpu.CompilerParams(vmem_limit_bytes=32 * MIB),
    )(out_in, grad_in, owned, small)


def rotary_tables():
    half = ROT_DIM // 2
    freqs = np.power(np.float32(10000.0), np.float32(-2.0) * np.arange(half, dtype=np.float32) / np.float32(ROT_DIM))
    angles = np.arange(1024, dtype=np.float32)[:, None] * freqs.astype(np.float32)[None, :]
    cosine, sine = np.cos(angles), np.sin(angles)
    ones = np.ones((1024, HEAD_DIM - ROT_DIM), np.float32)
    zero = np.zeros((1024, half), np.float32)
    cos_row = np.concatenate([cosine, cosine, ones], axis=1)
    left = np.concatenate([-sine, zero, ones * 0.0], axis=1)
    right = np.concatenate([zero, sine, ones * 0.0], axis=1)
    return np.stack([np.tile(t, (1, 2)) for t in (cos_row, left, right)]).astype(np.float32)


def place(values, owner, count):
    each = values.shape[0]
    spots = jnp.arange(count) // each
    return jnp.where(spots == owner, jnp.tile(values, count // each), jnp.zeros((), values.dtype))


def local(
    block_in,
    cotangent,
    attn_gain,
    attn_bias,
    mlp_gain,
    mlp_bias,
    qkv_weight,
    qkv_bias,
    proj_weight,
    proj_bias,
    up_weight,
    up_bias,
    down_weight,
    down_bias,
):
    dp = lax.axis_index("dp")
    me = lax.axis_index("seq")

    def quarter(array, axis):
        return lax.dynamic_index_in_dim(array, me, axis, keepdims=False)

    qkv = quarter(qkv_weight.reshape(24, 4, 3, 3, HEAD_DIM), 1)
    w_qk = qkv[:, :, :2, :].reshape(24, 384)
    w_v = qkv[:, :, 2, :].reshape(24, 192)
    w_p = quarter(proj_weight.reshape(24, 4, 192), 1)
    w_u = quarter(up_weight.reshape(24, 32, 4, 24), 2).reshape(24, 2, 384).transpose(1, 0, 2)
    w_d = quarter(down_weight.reshape(4, 24, 2, 384), 0).transpose(1, 0, 2)
    w_a = jnp.concatenate(
        [w_u, w_d, w_qk[None], jnp.concatenate([w_v, w_p], axis=1)[None]], axis=0
    )
    b_qkv = quarter(place(qkv_bias, dp, 2304).reshape(4, 3, 3, HEAD_DIM), 0)
    b_qkv = jnp.concatenate(
        [b_qkv[:, :2].reshape(384), b_qkv[:, 2].reshape(192), jnp.zeros((192,), BF)]
    )
    b_u = quarter(place(up_bias, dp, 3072).reshape(32, 4, 24), 1).reshape(768)
    rows = [
        place(v, dp, 768)
        for v in (attn_gain, attn_bias, mlp_gain, mlp_bias, proj_bias, down_bias)
    ]
    vec_in = jnp.concatenate([jnp.stack(rows + [b_qkv, b_u]), jnp.zeros((8, 768), BF)])
    out, grad, owned, small = whole(
        block_in.reshape(256, WIDTH),
        cotangent.reshape(256, WIDTH),
        w_a,
        vec_in,
        jnp.asarray(rotary_tables()),
    )
    results = finish(out, grad, owned, small)
    shapes = [(1, 256, WIDTH)] * 2 + [(24,)] * 4
    shapes += [(24, 2304), (72,), (24, 768), (24,), (24, 3072), (96,), (96, 768), (24,)]
    return tuple(value.reshape(size) for value, size in zip(results, shapes))


def solution(mesh):
    tokens = P("dp", "seq", None)
    in_specs = (tokens, tokens) + (P("dp"),) * 4 + (P("dp", None), P("dp")) * 4
    return jax.shard_map(
        local, mesh=mesh, in_specs=in_specs, out_specs=in_specs, check_vma=False
    )
```

time: 1380 us -> 128 us (0.09)
  waiting for transfers between devices: 747 us -> 0 us
  blocking collectives: 390 us -> 0 us
  Pallas kernels: 0 us -> 108 us
  matrix products: 68.2 us -> 0 us
  starting transfers between devices: 56.3 us -> 0 us
  other arithmetic: 38.6 us -> 0.95 us
  local copies, waits for them, and re-layouts: 51.2 us -> 17.6 us
  between operations: 19 us -> 0.92 us
    reduce_scatter x4 -> x0, waiting for transfers between devices: 444 us -> none  [the longest x1 170 us: local(): lax.psum_scatter(local_grads[10].astype(jnp.bfloat16), 'dp', scatter_dime...]
    unnamed x2 -> x0, blocking collectives: 267 us -> none
    all_gather x4 -> x0, waiting for transfers between devices: 247 us -> none  [the longest x1 133 us: local(): lax.all_gather(shards[10], 'dp', axis=0, tiled=True)]
    pallas_call x0 -> x2, Pallas kernels: none -> 108 us  [the longest x1 105 us: whole(): pl.pallas_call(whole_kernel, name='whole', out_shape=outs, in_specs=[vmem...]
    all_to_all x2 -> x0, blocking collectives: 82.9 us -> none  [the longest x1 46.5 us: local(): lax.all_to_all(as_sent(grad_packed.reshape(seqs_here, full_len, 1, heads_...]
    dot_general x24 -> x0, matrix products: 68.2 us -> none  [the longest x4 13.4 us: outer_sum(): jnp.einsum('rd,re->de', flat_rows(left), flat_rows(right), preferred_elem...]
    all_to_all x2 -> x0, starting transfers between devices: 55.4 us -> none  [the longest x1 30.5 us: local(): lax.all_to_all(grad_att_tokens.reshape(seqs_here, local_len, groups, head...]
    psum x1 -> x0, blocking collectives: 39.4 us -> none  [local(): lax.psum(owned[0].astype(jnp.bfloat16), 'seq').astype(jnp.float32)]
  transfers between devices with their start and end apart: 11 -> 0, of which waited for: 7 -> 0; matrix products, arithmetic and copies ran while one was open for 11% -> 0% of each run, Pallas kernels for 0% -> 0%
where the time goes in v2:
time: 128 us; the launch traced here: 127 us
  Pallas kernels  108 us (84%)
  local copies, waits for them, and re-layouts  17.6 us (14%)
    pallas_call x1, Pallas kernels, whole(): pl.pallas_call(whole_kernel, name='whole', out_shape=outs, in_specs=[vmem...  105 us
    another operation x15, local copies, waits for them, and re-layouts, place(): jnp.tile(values, count // each)  6.07 us
    unnamed x12, local copies, waits for them, and re-layouts  3.91 us
    pallas_call x1, Pallas kernels, finish(): pl.pallas_call(finish_kernel, name='finish', out_shape=outs, in_specs=[vm...  2.87 us

profile of v2, /device:TPU:1, one launch (start us, length us, event | category | flops | bytes accessed | tf_op | source)
XLA Modules:
  0.0 127.5 jit_solution(14564550812857506618)
XLA Ops:
  0.6 0.0 copy-start.4
  0.7 0.8 tile.86
  1.4 0.7 tile.32
  2.1 0.1 tile.33
  2.2 0.7 tile.34
  2.9 0.1 tile.35
  3.0 0.7 tile.36
  3.7 0.1 tile.37
  3.8 0.7 tile.38
  4.4 0.1 tile.39
  4.5 0.7 tile.84
  5.2 0.1 tile.85
  5.3 0.7 tile.80
  6.0 0.1 tile.81
  6.1 0.7 tile.82
  6.7 0.1 tile.83
  6.9 0.1 reshape.216
  7.0 0.1 reshape_squeeze.7
  7.1 0.1 pad_maximum_fusion.1
  7.2 0.9 reshape.215
  8.2 0.1 stack_reshape.3
  8.3 1.2 concatenate.15.vec_in
  9.5 0.9 reshape.213
  10.5 1.1 reshape.214
  11.8 0.1 broadcast_in_dim_reshape.3
  11.9 0.1 reshape_squeeze.6
  12.0 0.1 maximum_bitcast_fusion
  12.1 0.0 copy-done.4
  12.1 1.2 reshape.211
  13.3 1.3 %dynamic-slice_reduce_fusion = bf16[24,32,24]{2,1,0:T(8,128)(2,1)S(1)} fusion(bf16[24,32,4,24]{3,2,1,0:T(4,128)(2,1)S(1)} %reshape.211, s32[]{:T(128)S(6)} %select_n.134), kind=kLoop, calls=%fused_computation | loop fusion | bytes 73732 | tf_op jit(solution)/shard_map/jit(dynamic_index_in_dim)/dynamic_slice | solution.py:901
  14.6 0.2 reshape.212
  14.9 0.7 pad_maximum_fusion.w_a
  15.5 105.1 %whole.1 = (bf16[256,768]{1,0:T(8,128)(2,1)}, bf16[256,768]{1,0:T(8,128)(2,1)}, bf16[4,6,24,384]{3,2,1,0:T(8,128)(2,1)}, f32[4,8,768]{2,1,0:T(8,128)}) custom-call(bf16[256,768]{1,0:T(8,128)(2,1)} %bitcast.34, bf16[256,768]{1,0:T(8,128)(2,1)} %bitcast.35, bf16[6,24,384]{2,1,0:T(8,128)(2,1)} %pad_maximum_fusion.w_a, bf16[16,768]{1,0:T(8,128)(2,1)} %concatenate.15.vec_in, ...), custom_call_target="tpu_custom_call" | custom-call | tf_op jit(solution)/shard_map/whole/pallas_call | solution.py:746
  120.7 0.0 copy-start
  120.7 1.0 copy-done
  121.7 0.0 copy-start.1
  121.7 1.0 copy-done.1
  122.7 0.0 copy-start.2
  122.7 1.0 copy-done.2
  123.7 0.0 copy-start.3
  123.7 0.9 copy-done.3
  124.6 2.9 %finish.1 = (bf16[256,768]{1,0:T(8,128)(2,1)}, bf16[256,768]{1,0:T(8,128)(2,1)}, f32[1,24]{1,0:T(1,128)}, f32[1,24]{1,0:T(1,128)}, f32[1,24]{1,0:T(1,128)}, /*in...) custom-call(bf16[256,768]{1,0:T(8,128)(2,1)S(1)} %copy-done.1, ...), custom_call_target="tpu_custom_call" | custom-call | tf_op jit(solution)/shard_map/finish/pallas_call | solution.py:852
  (24 shorter events, 0.4 us)
Async XLA Ops:
  0.6 11.4 %copy-start.4 = (bf16[24,3072]{1,0:T(8,128)(2,1)S(1)}, bf16[24,3072]{1,0:T(8,128)(2,1)}, u32[]{:S(2)}) copy-start(bf16[24,3072]{1,0:T(8,128)(2,1)} %param.25) | copy-start | bytes 442372
  120.7 1.0 copy-start
  121.7 1.0 copy-start.1
  122.7 1.0 copy-start.2
  123.7 0.9 copy-start.3

commit v3 on v2

--- a/solution.py
+++ b/solution.py
@@ -62,11 +62,10 @@
     return lax.dot_general(left, right, (((0,), (0,)), ((), ())), preferred_element_type=F32)
 
 
-def greet(targets):
-    barrier = pltpu.get_barrier_semaphore()
-    for target in targets:
-        pl.semaphore_signal(barrier, inc=1, device_id=target, device_id_type=MESH)
-    pl.semaphore_wait(barrier, len(targets))
+def one_hot(rows, cols, chosen):
+    row = lax.broadcasted_iota(jnp.int32, (rows, cols), 0)
+    col = lax.broadcasted_iota(jnp.int32, (rows, cols), 1)
+    return chosen(row, col).astype(F32).astype(BF)
 
 
 def weight_rows(ref):
@@ -85,13 +84,24 @@
 def whole_kernel(
     x_in,
     g_in,
-    w_a,
-    vec_in,
-    tab,
+    qkv_weight,
+    proj_weight,
+    up_weight,
+    down_weight,
+    vec_raw,
+    tab_in,
     block_out,
     input_grad,
     owned,
     small,
+    qkv_own,
+    proj_own,
+    up_own,
+    down_own,
+    vec_own,
+    tab,
+    w_a,
+    vec_in,
     weights,
     vecs,
     z_a,
@@ -105,13 +115,17 @@
     in_mlp,
     in_mlp_t,
     activ,
-    low_grad,
+    activ_t,
     ob_part,
     gim_part,
     grads,
     p_send,
     p_recv,
     p_rows,
+    p_far,
+    p_far_rows,
+    att_send,
+    att_recv,
     qk_rows,
     vd_rows,
     dk_acc,
@@ -127,13 +141,13 @@
     kept,
     z_send,
     z_recv,
-    sums,
     swap_f,
     swap_r,
     far_b,
     far_r,
     small_b,
     small_r,
+    load_sem,
     pair_ss,
     pair_rs,
     tok_ss,
@@ -170,7 +184,10 @@
     z_pair = device(x, y, z_hi * 2 + 1 - z_lo, core)
     group = [sibling, far, cross]
     group_ids = [z_hi * 2 + 1 - core, (1 - z_hi) * 2 + core, (1 - z_hi) * 2 + 1 - core]
-    greet(x_peers + y_peers + group + [z_pair])
+    barrier = pltpu.get_barrier_semaphore()
+    everyone = x_peers + y_peers + group + [z_pair]
+    for target in everyone:
+        pl.semaphore_signal(barrier, inc=1, device_id=target, device_id_type=MESH)
 
     def token_rows(index):
         return pl.ds(pl.multiple_of(index * 256, 256), 256)
@@ -178,6 +195,85 @@
     def start(copies):
         for item in copies:
             item.start()
+
+    mine = token_rows(me)
+    theirs = token_rows(group_ids[1])
+    loads = [
+        pltpu.make_async_copy(source, held, load_sem.at[k])
+        for k, (source, held) in enumerate(
+            (
+                (up_weight, up_own),
+                (down_weight, down_own),
+                (vec_raw, vec_own),
+                (qkv_weight, qkv_own),
+                (proj_weight, proj_own),
+                (x_in, xx.at[mine]),
+                (g_in, gg.at[mine]),
+                (tab_in, tab),
+            )
+        )
+    ]
+    for item in loads:
+        item.start()
+
+    def of_quarter(parts):
+        value = parts[3]
+        for k in (2, 1, 0):
+            value = jnp.where(me == k, parts[k], value)
+        return value
+
+    loads[0].wait()
+    chosen = one_hot(
+        384,
+        96,
+        lambda row, col: row
+        == col
+        + 24 * me
+        + 72 * ((col >= 24).astype(jnp.int32) + (col >= 48).astype(jnp.int32) + (col >= 72).astype(jnp.int32)),
+    )
+    for b in range(2):
+        w_a[b] = jnp.concatenate(
+            [dot(up_own[:, k * 384 : k * 384 + 384], chosen) for k in range(4 * b, 4 * b + 4)],
+            axis=1,
+        ).astype(BF)
+    loads[1].wait()
+    picked = dot(one_hot(24, 96, lambda row, col: col == row + 24 * me), down_own[...])
+    w_a[2] = picked[:, :384].astype(BF)
+    w_a[3] = picked[:, 384:].astype(BF)
+    loads[2].wait()
+    owner = lax.axis_index("dp")
+    raw = vec_own[...].astype(F32)
+    up_bias = of_quarter([raw[7:8, 24 * k : 24 * k + 24] for k in range(4)])
+    eight = jnp.concatenate([raw[:7, :24], up_bias], axis=0).astype(BF)
+    placed = dot(eight, one_hot(24, WIDTH, lambda row, col: col == row + 24 * owner))
+    start_at = jnp.where(x == me, 72 * lax.rem(owner, 8), 2 * WIDTH)
+    placed_qkv = dot(
+        jnp.broadcast_to(raw[6:7, :72], (8, 72)).astype(BF),
+        one_hot(72, WIDTH, lambda row, col: col == row + start_at),
+    )
+    vec_in[...] = jnp.concatenate(
+        [placed[:6], placed_qkv[:1], placed[7:], jnp.zeros((8, WIDTH), F32)], axis=0
+    ).astype(BF)
+    loads[3].wait()
+    loads[4].wait()
+    qkv_f = qkv_own[...].astype(F32)
+    proj_f = proj_own[...].astype(F32)
+    w_a[QK] = jnp.concatenate(
+        [
+            of_quarter([qkv_f[:, 576 * k + 192 * h : 576 * k + 192 * h + 128] for k in range(4)])
+            for h in range(3)
+        ],
+        axis=1,
+    ).astype(BF)
+    w_a[VP] = jnp.concatenate(
+        [
+            of_quarter([qkv_f[:, 576 * k + 192 * h + 128 : 576 * k + 192 * h + 192] for k in range(4)])
+            for h in range(3)
+        ]
+        + [of_quarter([proj_f[:, 192 * k : 192 * k + 192] for k in range(4)])],
+        axis=1,
+    ).astype(BF)
+    pl.semaphore_wait(barrier, len(everyone))
 
     pair = [copy_to(vec_in, z_v, pair_ss.at[0], pair_rs.at[0], z_pair)]
     for k in range(3):
@@ -187,8 +283,6 @@
         )
     start([pair[1], pair[0], pair[2], pair[3]])
 
-    mine = token_rows(me)
-    theirs = token_rows(group_ids[1])
     tokens = []
     for k, (source, held) in enumerate(((x_in, xx), (g_in, gg))):
         tokens.append(
@@ -201,8 +295,6 @@
     for k in range(2):
         tokens[k][1].start()
         tokens[k][0].start()
-    xx[mine, :] = x_in[...]
-    gg[mine, :] = g_in[...]
 
     def assemble(i):
         own = w_a[i].astype(F32)
@@ -248,6 +340,16 @@
             inv_std = lax.rsqrt(jnp.mean(center * center, axis=-1, keepdims=True) + EPSILON)
             normed[rows, :] = center * inv_std
 
+    def norm_inputs(index):
+        rows = token_rows(index)
+        values = normed[rows, :]
+        attn_rows = (values * vec[0:1, :] + vec[1:2, :]).astype(BF)
+        mlp_rows = (values * vec[2:3, :] + vec[3:4, :]).astype(BF)
+        in_attn[rows, :] = attn_rows
+        in_mlp[rows, :] = mlp_rows
+        in_attn_t[:, rows] = attn_rows.T
+        in_mlp_t[:, rows] = mlp_rows.T
+
     pair[1].wait_recv()
     assemble(0)
     assemble(1)
@@ -259,47 +361,37 @@
     assemble(2)
     assemble(3)
     start(gather(2, 1) + gather(3, 1))
+    for i in (0, 1, N_BLOCK):
+        arrived(i, 1)
+        start(gather(i, 2))
     pair[3].wait_recv()
     assemble(4)
     assemble(5)
     start(gather(4, 1) + gather(5, 1))
+    loads[5].wait()
     layer_norm(me)
-    for i in (0, 1, N_BLOCK, 2, 3, 4, 5):
+    for i in (2, 3, 4, 5):
         arrived(i, 1)
         start(gather(i, 2))
     tokens[0][0].wait_recv()
     layer_norm(group_ids[0])
-    tokens[0][1].wait_recv()
-    tokens[0][2].start()
-    layer_norm(group_ids[1])
-    tokens[0][2].wait_recv()
-    layer_norm(group_ids[2])
     arrived(N_BLOCK, 2)
     total = jnp.zeros((16, WIDTH), F32)
     for i in range(4):
         for j in range(4):
             total = total + vecs[i, j].astype(F32)
     vec[...] = total
-
-    @pl.loop(0, 4)
-    def _(step):
-        rows = token_rows(step)
-        values = normed[rows, :]
-        attn_rows = (values * vec[0:1, :] + vec[1:2, :]).astype(BF)
-        mlp_rows = (values * vec[2:3, :] + vec[3:4, :]).astype(BF)
-        in_attn[rows, :] = attn_rows
-        in_mlp[rows, :] = mlp_rows
-        in_attn_t[:, rows] = attn_rows.T
-        in_mlp_t[:, rows] = mlp_rows.T
-
-    tokens[1][1].wait_recv()
-    tokens[1][2].start()
-    tokens[1][0].wait_recv()
+    norm_inputs(me)
+    norm_inputs(group_ids[0])
+    tokens[0][1].wait_recv()
+    tokens[0][2].start()
+    layer_norm(group_ids[1])
+    norm_inputs(group_ids[1])
+    tokens[0][2].wait_recv()
+    layer_norm(group_ids[2])
+    norm_inputs(group_ids[2])
     arrived(0, 2)
     arrived(1, 2)
-    arrived(2, 2)
-    arrived(3, 2)
-    tokens[1][2].wait_recv()
 
     def first_copies(i):
         ref = grads.at[i]
@@ -373,10 +465,10 @@
         pair_copy(i).wait_recv()
         owned[me, i] = (kept[i] + z_recv[i].astype(F32)).astype(BF)
 
-    def p_copies(sent, received, number):
+    def p_copies(sent, received, number, turn=0):
         return [
             copy_to(
-                sent.at[group_ids[k]],
+                sent.at[around(group_ids[k], turn)],
                 received.at[me],
                 p_ss.at[number, k],
                 p_rs.at[number, k],
@@ -395,69 +487,103 @@
                 group[k],
             ).wait_recv()
 
-    for b in range(2):
-        weight_up = weight_rows(weights.at[b])
-        down = [
-            weights[2 + half, 2 * b : 2 * b + 2].reshape(384, 384) for half in range(2)
-        ]
-
-        @pl.loop(0, 4)
-        def _(step):
-            rows = token_rows(step)
-            up_pre = dot(in_mlp[rows, :], weight_up) + vec[7:8, b * 384 : b * 384 + 384]
+    def swap(k):
+        return copy_to(swap_f.at[k], swap_r.at[k], swap_ss.at[k], swap_rs.at[k], sibling)
+
+    def far_swap(k):
+        return copy_to(far_b.at[k], far_r.at[k], swap_ss.at[4 + k], swap_rs.at[4 + k], far)
+
+    def att_copy(k):
+        return copy_to(
+            att_send.at[k], att_recv.at[k], swap_ss.at[6 + k], swap_rs.at[6 + k], far
+        )
+
+    @pl.loop(0, 4)
+    def _(step):
+        rows = token_rows(step)
+        for b in range(2):
+            cols = slice(b * 384, b * 384 + 384)
+            up_pre = dot(in_mlp[rows, :], weight_rows(weights.at[b])) + vec[7:8, cols]
             cdf = 0.5 * (1.0 + lax.erf(up_pre * (1.0 / math.sqrt(2.0))))
             act = (up_pre * cdf).astype(BF)
             density = jnp.exp(-0.5 * up_pre * up_pre) * (1.0 / math.sqrt(2.0 * math.pi))
-            slope = cdf + up_pre * density
-            grad_activ = dot_t(gg[rows, :384], down[0]) + dot_t(gg[rows, 384:], down[1])
-            grad_up = (grad_activ * slope).astype(BF)
-            activ[rows, :] = act
-            low_grad[rows, :] = grad_up
-            for half in range(2):
-                cols = slice(half * 384, half * 384 + 384)
-                out = dot(act, down[half])
-                if b:
-                    out = out + ob_part[rows, cols]
-                ob_part[rows, cols] = out
-            back = dot_t(grad_up, weight_up)
-            if b:
-                back = back + gim_part[rows, :]
-            gim_part[rows, :] = back
-
-        grads[b] = dot(in_mlp_t[...], low_grad[...]).astype(BF).reshape(4, 4, 48, 384)
+            activ[rows, cols] = act
+            activ_t[cols, rows] = act.T
+            swap_f[step, :, cols] = cdf + up_pre * density
+
+    def mlp_back(index):
+        rows = token_rows(index)
+        down = [weight_rows(weights.at[2 + half]) for half in range(2)]
+        grad_activ = dot_t(gg[rows, :384], down[0]) + dot_t(gg[rows, 384:], down[1])
+        grad_up = (grad_activ * swap_f[index]).astype(BF)
+        act = activ[rows, :]
+        activ[rows, :] = grad_up
+        for half in range(2):
+            cols = slice(half * 384, half * 384 + 384)
+            ob_part[rows, cols] = dot(act, down[half])
+        gim_part[rows, :] = dot_t(grad_up[:, :384], weight_rows(weights.at[0])) + dot_t(
+            grad_up[:, 384:], weight_rows(weights.at[1])
+        )
+
+    loads[6].wait()
+    tokens[1][0].wait_recv()
+    arrived(2, 2)
+    arrived(3, 2)
+
+    @pl.loop(0, 2)
+    def _(step):
+        mlp_back(z_hi * 2 + step)
+
+    tokens[1][1].wait_recv()
+    tokens[1][2].start()
+    arrived(VP, 2)
+    for k in range(4):
+        p_send[k] = weights[VP, k].reshape(192, 384)[:, 192:]
+    start(p_copies(p_send, p_recv, 0) + p_copies(p_send, p_far, 2, 2))
+    p_recv[me] = p_send[me]
+    p_far[me] = p_send[around(me, 2)]
+    tokens[1][2].wait_recv()
+    for half in range(2):
+        cols = slice(half * 384, half * 384 + 384)
+        grads[2 + half] = dot(activ_t[...], gg[:, cols]).astype(BF).reshape(4, 4, 48, 384)
+        start(first_copies(2 + half))
+
+    @pl.loop(0, 2)
+    def _(step):
+        mlp_back((1 - z_hi) * 2 + step)
+
+    for b in range(2):
+        cols = slice(b * 384, b * 384 + 384)
+        grads[b] = dot(in_mlp_t[...], activ[:, cols]).astype(BF).reshape(4, 4, 48, 384)
         start(first_copies(b))
-        small_b[6:7, b * 384 : b * 384 + 384] = jnp.sum(
-            low_grad[...].astype(F32), axis=0, keepdims=True
-        )
-        activ_t = activ[...].T
-        for half in range(2):
-            grad_down = dot(activ_t, gg[:, half * 384 : half * 384 + 384]).astype(BF)
-            grads[2 + half, 2 * b : 2 * b + 2] = grad_down.reshape(2, 4, 48, 384)
-        if b == 0:
-            arrived(VP, 2)
-            for k in range(4):
-                p_send[k] = weights[VP, k].reshape(192, 384)[:, 192:]
-            start(p_copies(p_send, p_recv, 0))
-            p_recv[me] = p_send[me]
-    start(first_copies(2) + first_copies(3))
-
+    swap_f[1] = ob_part[token_rows(group_ids[2]), :]
+    swap(1).start()
+    small_b[6:7, :] = jnp.sum(activ[...].astype(F32), axis=0, keepdims=True)
     grad_in = gim_part[...]
     small_b[2:3, :] = jnp.sum(grad_in * normed[...], axis=0, keepdims=True)
     small_b[3:4, :] = jnp.sum(grad_in, axis=0, keepdims=True)
-    small_b[4:5, :] = jnp.sum(g_in[...].astype(F32), axis=0, keepdims=True)
+    small_b[4:5, :] = jnp.sum(gg[mine, :].astype(F32), axis=0, keepdims=True)
     small_b[7:8, :] = jnp.zeros((1, WIDTH), F32)
 
     p_arrived(p_send, p_recv, 0)
+    p_arrived(p_send, p_far, 2)
     for k in range(4):
         p_rows[:, k * 192 : k * 192 + 192] = p_recv[k]
+        p_far_rows[:, k * 192 : k * 192 + 192] = p_far[k]
     arrived(QK, 2)
+    loads[7].wait()
 
     @pl.loop(0, 4)
     def _(step):
         rows = token_rows(step)
         activations = in_attn[rows, :]
-        pre = dot(activations, weight_rows(weights.at[QK])) + vec[6:7, :384]
-        value_pre = dot(activations, weight_rows(weights.at[VP])[:, :192]) + vec[6:7, 384:576]
+        bias = vec[6:7, :576]
+        pre = dot(activations, weight_rows(weights.at[QK])) + jnp.concatenate(
+            [bias[:, 192 * h : 192 * h + 128] for h in range(3)], axis=1
+        )
+        value_pre = dot(activations, weight_rows(weights.at[VP])[:, :192]) + jnp.concatenate(
+            [bias[:, 192 * h + 128 : 192 * h + 192] for h in range(3)], axis=1
+        )
         value_pre = value_pre.astype(BF)
         grad_att = dot_t(gg[rows, :], p_rows[...]).astype(BF)
         for head in range(3):
@@ -509,17 +635,25 @@
             - pltpu.roll(part, 8, 1) * tab[2]
         ).astype(BF)
 
+    swap(1).wait_recv()
+    far_b[1] = (ob_part[token_rows(group_ids[1]), :] + swap_r[1]).astype(BF)
+    far_swap(1).start()
+    far_rows = pl.ds(pl.multiple_of((1 - z_hi) * 512, 512), 512)
     attend(0)
+    first_sum(2)
+    first_sum(3)
+    attend(1)
+    att_send[0] = att[far_rows, 0:128]
+    att_copy(0).start()
     first_sum(0)
     first_sum(1)
-    attend(1)
-    first_sum(2)
-    first_sum(3)
+    second_sum(2)
+    second_sum(3)
+    attend(2)
+    att_send[1] = jnp.concatenate([att[far_rows, 128:192], jnp.zeros((512, 64), BF)], axis=1)
+    att_copy(1).start()
     second_sum(0)
     second_sum(1)
-    attend(2)
-    second_sum(2)
-    second_sum(3)
 
     def grad_chunk(index, number):
         rows = token_rows(index)
@@ -537,18 +671,16 @@
 
     def out_chunk(index):
         rows = token_rows(index)
-        return ob_part[rows, :] + dot(att[rows, :], p_rows[...])
-
-    def swap(k):
-        return copy_to(swap_f.at[k], swap_r.at[k], swap_ss.at[k], swap_rs.at[k], sibling)
-
-    def far_swap(k):
-        return copy_to(far_b.at[k], far_r.at[k], swap_ss.at[4 + k], swap_rs.at[4 + k], far)
-
+        near = pl.ds(pl.multiple_of((index - 2 * z_hi) * 256, 256), 256)
+        far_heads = jnp.concatenate([att_recv[0, near, :], att_recv[1, near, 0:64]], axis=1)
+        return (
+            ob_part[rows, :] + dot(att[rows, :], p_rows[...]) + dot(far_heads, p_far_rows[...])
+        )
+
+    grads[QK] = dot(in_attn_t[...], grad_qk[...]).astype(BF).reshape(4, 4, 48, 384)
+    start(first_copies(QK))
     swap_f[0] = grad_chunk(group_ids[2], 0)
     swap(0).start()
-    grads[QK] = dot(in_attn_t[...], grad_qk[...]).astype(BF).reshape(4, 4, 48, 384)
-    start(first_copies(QK))
     grad_p = dot_a(att[...], gg[...]).astype(BF)
     for k in range(4):
         pg_send[k] = grad_p[:, k * 192 : k * 192 + 192]
@@ -558,8 +690,6 @@
     swap(0).wait_recv()
     far_b[0] = (near_sum + swap_r[0]).astype(BF)
     far_swap(0).start()
-    swap_f[1] = out_chunk(group_ids[2])
-    swap(1).start()
     for i in range(4):
         third_sum(i)
     start(share_copies(0))
@@ -570,16 +700,14 @@
             [grad_value_w[k * 192 : k * 192 + 192], pg_recv[k]], axis=1
         ).reshape(4, 48, 384)
     start(first_copies(VP))
-    out_sum = out_chunk(group_ids[1])
-    swap(1).wait_recv()
-    far_b[1] = (out_sum + swap_r[1]).astype(BF)
-    far_swap(1).start()
     swap_f[2] = grad_chunk(group_ids[0], 2)
     swap(2).start()
+    att_copy(0).wait_recv()
+    att_copy(1).wait_recv()
     swap_f[3] = out_chunk(group_ids[0])
     swap(3).start()
-    sums[0] = grad_chunk(me, 3)
-    sums[1] = out_chunk(me)
+    gim_part[mine, :] = grad_chunk(me, 3)
+    ob_part[mine, :] = out_chunk(me)
     small_b[5:6, 0:384] = jnp.sum(grad_qk[...].astype(F32), axis=0, keepdims=True)
     small_b[5:6, 384:576] = jnp.sum(grad_v[...].astype(F32), axis=0, keepdims=True)
     small_b[5:6, 576:768] = jnp.zeros((1, 192), F32)
@@ -628,13 +756,13 @@
 
     swap(2).wait_recv()
     far_swap(0).wait_recv()
-    values = x_in[...].astype(F32)
+    values = xx[mine, :].astype(F32)
     center = values - jnp.mean(values, axis=-1, keepdims=True)
     inv_std = lax.rsqrt(jnp.mean(center * center, axis=-1, keepdims=True) + EPSILON)
     norm_rows = center * inv_std
-    grad_norm = sums[0] + swap_r[2] + far_r[0].astype(F32)
+    grad_norm = gim_part[mine, :] + swap_r[2] + far_r[0].astype(F32)
     input_grad[...] = (
-        g_in[...].astype(F32)
+        gg[mine, :].astype(F32)
         + inv_std
         * (
             grad_norm
@@ -645,7 +773,7 @@
     swap(3).wait_recv()
     far_swap(1).wait_recv()
     block_out[...] = (
-        values + sums[1] + swap_r[3] + far_r[1].astype(F32) + (vec[4:5, :] + vec[5:6, :])
+        values + ob_part[mine, :] + swap_r[3] + far_r[1].astype(F32) + (vec[4:5, :] + vec[5:6, :])
     ).astype(BF)
 
     share_arrived(0)
@@ -663,16 +791,16 @@
         sent += gather(i, 1) + gather(i, 2)
     for i in range(N_BLOCK):
         sent += first_copies(i) + second_copies(i) + [pair_copy(i)]
-    sent += p_copies(p_send, p_recv, 0) + p_copies(pg_send, pg_recv, 1)
+    sent += p_copies(p_send, p_recv, 0) + p_copies(p_send, p_far, 2, 2) + p_copies(pg_send, pg_recv, 1)
     sent += share_copies(0) + share_copies(1) + [small_share(k) for k in range(3)]
-    sent += [swap(k) for k in range(4)] + [far_swap(k) for k in range(2)]
+    sent += [swap(k) for k in range(4)] + [far_swap(k) for k in range(2)] + [att_copy(k) for k in range(2)]
     for number in range(3):
         sent += small_copies(number)
     for item in sent:
         item.wait_send()
 
 
-def whole(x_in, g_in, w_a, vec_in, tab):
+def whole(x_in, g_in, qkv_weight, proj_weight, up_weight, down_weight, vec_raw, tab):
     shape = jax.ShapeDtypeStruct
     outs = (
         shape((256, WIDTH), BF),
@@ -684,6 +812,14 @@
     vmem = pl.BlockSpec(memory_space=pltpu.VMEM)
     rows = 1024
     buffers = [
+        ((24, 2304), BF),
+        ((24, 768), BF),
+        ((24, 3072), BF),
+        ((96, 768), BF),
+        ((8, 128), BF),
+        ((3, rows, 128), F32),
+        ((N_BLOCK, 24, 384), BF),
+        ((16, WIDTH), BF),
         ((N_BLOCK, 4, 4, 48, 384), BF),
         ((4, 4, 16, WIDTH), BF),
         ((N_BLOCK, 24, 384), BF),
@@ -696,14 +832,18 @@
         ((WIDTH, rows), BF),
         ((rows, WIDTH), BF),
         ((WIDTH, rows), BF),
-        ((rows, 384), BF),
-        ((rows, 384), BF),
+        ((rows, WIDTH), BF),
+        ((WIDTH, rows), BF),
         ((rows, WIDTH), F32),
         ((rows, WIDTH), F32),
         ((N_BLOCK, 4, 4, 48, 384), BF),
         ((4, 192, 192), BF),
         ((4, 192, 192), BF),
         ((192, WIDTH), BF),
+        ((4, 192, 192), BF),
+        ((192, WIDTH), BF),
+        ((2, 512, 128), BF),
+        ((2, 512, 128), BF),
         ((3, rows, 128), BF),
         ((3, rows, 128), BF),
         ((rows, HEAD_DIM), F32),
@@ -719,7 +859,6 @@
         ((N_BLOCK, 24, 384), F32),
         ((N_BLOCK, 24, 384), BF),
         ((N_BLOCK, 24, 384), BF),
-        ((2, 256, WIDTH), F32),
         ((4, 256, WIDTH), F32),
         ((4, 256, WIDTH), F32),
         ((2, 256, WIDTH), BF),
@@ -732,35 +871,35 @@
         (2, 3),
         (N_BLOCK + 1, 3),
         (N_BLOCK + 1, 3),
-        (2, 3),
+        (3, 3),
         (N_BLOCK, 3),
         (N_BLOCK, 3),
         (N_BLOCK,),
         (2, 3),
-        (6,),
+        (8,),
         (4, 3),
     ]
-    scratch = [pltpu.VMEM(*item) for item in buffers]
+    scratch = [pltpu.VMEM(*item) for item in buffers] + [dma((8,))]
     for item in sems:
         scratch += [dma(item), dma(item)]
     return pl.pallas_call(
         whole_kernel,
         name="whole",
         out_shape=outs,
-        in_specs=[vmem] * 5,
+        in_specs=[pl.BlockSpec(memory_space=pltpu.HBM)] * 8,
         out_specs=(vmem,) * len(outs),
         scratch_shapes=scratch,
         compiler_params=pltpu.CompilerParams(
             collective_id=0, has_side_effects=True, vmem_limit_bytes=60 * MIB
         ),
-    )(x_in, g_in, w_a, vec_in, tab)
+    )(x_in, g_in, qkv_weight, proj_weight, up_weight, down_weight, vec_raw, tab)
 
 
 def finish_kernel(
     out_in,
     grad_in,
-    owned,
-    small,
+    owned_in,
+    small_in,
     block_out,
     input_grad,
     attn_gain_g,
@@ -775,9 +914,19 @@
     up_bias_g,
     down_g,
     down_bias_g,
+    owned,
+    small,
+    sems,
 ):
-    block_out[...] = out_in[...]
-    input_grad[...] = grad_in[...]
+    copies = [
+        pltpu.make_async_copy(owned_in, owned, sems.at[0]),
+        pltpu.make_async_copy(small_in, small, sems.at[1]),
+        pltpu.make_async_copy(out_in, block_out, sems.at[2]),
+        pltpu.make_async_copy(grad_in, input_grad, sems.at[3]),
+    ]
+    for item in copies:
+        item.start()
+    copies[0].wait()
     up_parts = []
     for g in range(4):
         qk = owned[g, QK].astype(F32)
@@ -798,6 +947,7 @@
             [up_parts[g][d // 16][:, at : at + 24] for g in range(4)], axis=1
         )
 
+    copies[1].wait()
     dp = lax.axis_index("dp")
     totals = small[0] + small[1] + small[2] + small[3]
     rows = jnp.concatenate(
@@ -828,6 +978,8 @@
             pieces.append(small[g, 5:6, 384 + head * 64 : 384 + head * 64 + 64])
     bias = jnp.concatenate(pieces, axis=1)
     qkv_bias_g[...] = pick(jnp.broadcast_to(bias, (8, 2304)), 72)[0:1]
+    copies[2].wait()
+    copies[3].wait()
 
 
 def finish(out_in, grad_in, owned, small):
@@ -849,13 +1001,19 @@
         shape((1, 24), F32),
     )
     vmem = pl.BlockSpec(memory_space=pltpu.VMEM)
+    anywhere = pl.BlockSpec(memory_space=pltpu.HBM)
     return pl.pallas_call(
         finish_kernel,
         name="finish",
         out_shape=outs,
-        in_specs=[vmem] * 4,
+        in_specs=[anywhere] * 4,
         out_specs=(vmem,) * len(outs),
-        compiler_params=pltpu.CompilerParams(vmem_limit_bytes=32 * MIB),
+        scratch_shapes=[
+            pltpu.VMEM((4, N_BLOCK, 24, 384), BF),
+            pltpu.VMEM((4, 8, WIDTH), F32),
+            pltpu.SemaphoreType.DMA((4,)),
+        ],
+        compiler_params=pltpu.CompilerParams(vmem_limit_bytes=60 * MIB),
     )(out_in, grad_in, owned, small)
 
 
@@ -870,12 +1028,6 @@
     left = np.concatenate([-sine, zero, ones * 0.0], axis=1)
     right = np.concatenate([zero, sine, ones * 0.0], axis=1)
     return np.stack([np.tile(t, (1, 2)) for t in (cos_row, left, right)]).astype(np.float32)
-
-
-def place(values, owner, count):
-    each = values.shape[0]
-    spots = jnp.arange(count) // each
-    return jnp.where(spots == owner, jnp.tile(values, count // each), jnp.zeros((), values.dtype))
 
 
 def local(
@@ -894,36 +1046,20 @@
     down_weight,
     down_bias,
 ):
-    dp = lax.axis_index("dp")
-    me = lax.axis_index("seq")
-
-    def quarter(array, axis):
-        return lax.dynamic_index_in_dim(array, me, axis, keepdims=False)
-
-    qkv = quarter(qkv_weight.reshape(24, 4, 3, 3, HEAD_DIM), 1)
-    w_qk = qkv[:, :, :2, :].reshape(24, 384)
-    w_v = qkv[:, :, 2, :].reshape(24, 192)
-    w_p = quarter(proj_weight.reshape(24, 4, 192), 1)
-    w_u = quarter(up_weight.reshape(24, 32, 4, 24), 2).reshape(24, 2, 384).transpose(1, 0, 2)
-    w_d = quarter(down_weight.reshape(4, 24, 2, 384), 0).transpose(1, 0, 2)
-    w_a = jnp.concatenate(
-        [w_u, w_d, w_qk[None], jnp.concatenate([w_v, w_p], axis=1)[None]], axis=0
-    )
-    b_qkv = quarter(place(qkv_bias, dp, 2304).reshape(4, 3, 3, HEAD_DIM), 0)
-    b_qkv = jnp.concatenate(
-        [b_qkv[:, :2].reshape(384), b_qkv[:, 2].reshape(192), jnp.zeros((192,), BF)]
-    )
-    b_u = quarter(place(up_bias, dp, 3072).reshape(32, 4, 24), 1).reshape(768)
-    rows = [
-        place(v, dp, 768)
-        for v in (attn_gain, attn_bias, mlp_gain, mlp_bias, proj_bias, down_bias)
-    ]
-    vec_in = jnp.concatenate([jnp.stack(rows + [b_qkv, b_u]), jnp.zeros((8, 768), BF)])
+    vec_raw = jnp.zeros((8, 128), BF)
+    for row, values in enumerate(
+        (attn_gain, attn_bias, mlp_gain, mlp_bias, proj_bias, down_bias, qkv_bias, up_bias)
+    ):
+        spare = ((row, 7 - row), (0, 128 - values.shape[0]))
+        vec_raw = vec_raw + jnp.pad(values[None, :], spare)
     out, grad, owned, small = whole(
         block_in.reshape(256, WIDTH),
         cotangent.reshape(256, WIDTH),
-        w_a,
-        vec_in,
+        qkv_weight,
+        proj_weight,
+        up_weight,
+        down_weight,
+        vec_raw,
         jnp.asarray(rotary_tables()),
     )
     results = finish(out, grad, owned, small)

time: 128 us -> 111 us (0.87)
  local copies, waits for them, and re-layouts: 17.6 us -> 0 us
    another operation x20 -> x0, local copies, waits for them, and re-layouts: 6.44 us -> none  [the longest x15 6.07 us: place(): jnp.tile(values, count // each)]
    reshape x7 -> x0, local copies, waits for them, and re-layouts: 4.49 us -> none  [the longest x1 1.23 us: local(): up_weight.reshape(24, 32, 4, 24)]
    unnamed x12 -> x0, local copies, waits for them, and re-layouts: 3.91 us -> none
    dynamic_slice x6 -> x0, local copies, waits for them, and re-layouts: 1.42 us -> none  [quarter(): return lax.dynamic_index_in_dim(array, me, axis, keepdims=False)]
    add x0 -> x1, other arithmetic: none -> 1.36 us  [local(): vec_raw = vec_raw + jnp.pad(values[None, :], spare)]
where the time goes in v3:
time: 111 us
  Pallas kernels  108 us (97%)
  other arithmetic  1.36 us (1%)
    pallas_call x1, Pallas kernels, whole(): pl.pallas_call(whole_kernel, name='whole', out_shape=outs, in_specs=[pl.B...  104 us
    pallas_call x1, Pallas kernels, finish(): pl.pallas_call(finish_kernel, name='finish', out_shape=outs, in_specs=[an...  4.67 us

profile of v3, /device:TPU:1, one launch (start us, length us, event | category | flops | bytes accessed | tf_op | source)
XLA Modules:
  0.0 110.5 jit_solution(5921316071006339680)
XLA Ops:
  0.6 1.4 %pad_add_fusion.vec_raw = bf16[8,128]{1,0:T(8,128)(2,1)} fusion(bf16[1,96]{1,0:T(2,128)(2,1)} %bitcast.22, bf16[1,72]{1,0:T(2,128)(2,1)} %bitcast.23, bf16[1,24]{1,0:T(2,128)(2,1)} %bitcast.24, bf16[1,24]{1,0:T(2,128)(2,1)} %bitcast.25, bf16[1,24]{1,0:T(2,128)(2,1)} %bitcast.26, bf16[1,24]{1,0:T(2,128)(2,1)} %bitcast.27, bf16[1,24]{1,0:T(2,128)(2,1)} %bitcast.28, ...), kind=kLoop, calls=%fused_computation | loop fusion | flops 16384 | bytes 2672 | tf_op jit(solution)/shard_map/add | solution.py:1054
  2.0 103.6 %whole.1 = (bf16[256,768]{1,0:T(8,128)(2,1)}, bf16[256,768]{1,0:T(8,128)(2,1)}, bf16[4,6,24,384]{3,2,1,0:T(8,128)(2,1)}, f32[4,8,768]{2,1,0:T(8,128)}) custom-call(bf16[256,768]{1,0:T(8,128)(2,1)} %bitcast.20, bf16[256,768]{1,0:T(8,128)(2,1)} %bitcast.21, bf16[24,2304]{1,0:T(8,128)(2,1)} %qkv_weight.1, bf16[24,768]{1,0:T(8,128)(2,1)} %proj_weight.1, ...), custom_call_target="tpu_custom_call" | custom-call | tf_op jit(solution)/shard_map/whole/pallas_call | solution.py:885
  105.7 4.7 %finish.1 = (bf16[256,768]{1,0:T(8,128)(2,1)}, bf16[256,768]{1,0:T(8,128)(2,1)}, f32[1,24]{1,0:T(1,128)}, f32[1,24]{1,0:T(1,128)}, f32[1,24]{1,0:T(1,128)}, /*in...) custom-call(bf16[256,768]{1,0:T(8,128)(2,1)} %get-tuple-element.32.o, ...), custom_call_target="tpu_custom_call" | custom-call | tf_op jit(solution)/shard_map/finish/pallas_call | solution.py:1005
